TPU v7x, 128 devices: a whole 4x4x4 slice. The times are simulated.
128 devices in a mesh: dp: 2 (over z_hi), latent: 64 (over z_lo, x, y, core).
Axes of the slice: x: 4, y: 4, z: 4 (z_hi: 2, z_lo: 2; z = z_hi * 2 + z_lo), core: 2. Of those that a mesh axis runs over, the one named last changes fastest.
Arguments:
- inputs: bfloat16 [1152, 4096], P('dp', 'latent'), may hold values from -36 to 36
- dictionary: float32 [16384, 4096], P('latent')
- offset: float32 [16384], P('latent'), may hold values from -3 to 3
- center: float32 [4096], P('latent'), may hold values from -3 to 3
- dict_mean: float32 [16384, 4096], P('latent'), may hold values from -0.12 to 0.12
- dict_var: float32 [16384, 4096], P('latent'), may hold values from 1e-05 to 0.001
- offset_mean: float32 [16384], P('latent'), may hold values from -0.12 to 0.12
- offset_var: float32 [16384], P('latent'), may hold values from 0.01 to 1000
- center_mean: float32 [4096], P('latent'), may hold values from -250 to 250
- center_var: float32 [4096], P('latent'), may hold values from 0.1 to 10000
Outputs:
- fresh_dict: float32 [16384, 4096], P('latent')
- fresh_offset: float32 [16384], P('latent')
- fresh_center: float32 [4096], P('latent')
- mean_dict: float32 [16384, 4096], P('latent')
- var_dict: float32 [16384, 4096], P('latent')
- mean_offset: float32 [16384], P('latent')
- var_offset: float32 [16384], P('latent')
- mean_center: float32 [4096], P('latent')
- var_center: float32 [4096], P('latent')
- loss_value: float32 [], replicated
All inputs are finite; a program needn't handle non-finite values.
Results may differ from a plain program's by a relative error of at most 0.0064.
Values may be sent and summed in bfloat16 or wider, within the bound.
A program may use at most 128 MiB of HBM per device.

v0:
```python
import jax
import jax.numpy as jnp
from jax import lax
from jax.experimental import pallas as pl
from jax.experimental.pallas import tpu as pltpu
from jax.sharding import PartitionSpec as P

STEP = 1000
sparsity_coeff = 5.0
beta_one = 0.9
beta_two = 0.999
learn_rate = 0.001
adam_eps = 1e-08
norm_eps = 1e-06

TOK = 1152
WIDTH = 4096
ROWS = 288
CHUNK = 144
PART = 48
MAIN, SIDE = 64, 16
LAT = 256
EARLY = 192
LATE = 384
VMEM_LIMIT = 40 * 1024 * 1024
F32 = jnp.float32
BF16 = jnp.bfloat16
MESH = pl.DeviceIdType.MESH


def adam_update(param, grad, mean, var):
    mean_new = beta_one * mean + (1.0 - beta_one) * grad
    var_new = beta_two * var + (1.0 - beta_two) * grad * grad
    rate = learn_rate / (1.0 - beta_one**STEP)
    scaled = var_new * (1.0 / (1.0 - beta_two**STEP))
    param_new = param - rate * mean_new / (scaled * lax.rsqrt(scaled) + adam_eps)
    return (param_new, mean_new, var_new)


def mod4(v):
    return lax.rem(v + 4, 4)


def dot(a, b):
    return jnp.dot(a, b, preferred_element_type=F32)


def dot_nt(a, b):
    return lax.dot_general(a, b, (((1,), (1,)), ((), ())), preferred_element_type=F32)


def kernel(
    inputs_hbm, center_hbm, offset_hbm, dict_ref,
    grad_ref, g_in, small_ref,
    inputs_ref, center_ref, offset_ref,
    weights, gx, ge, pre, dacc, acts, tmat0, tmat1, gacc,
    raw, raw_in, cen, cen_in, sm, sm_in, sums, sums_in,
    part, b0_out, b0_in, a0_out, a0_in, z_out, z_in,
    side, y_out, y_in, c1_out, c1_in, c2_out, c2_in,
    g_out,
    vx, vx_in, vy, vy_in, vz, vz_in,
    load_sem, pair_send, pair_recv,
    gx_send, gx_recv, ge_send, ge_recv, rs_send, rs_recv,
    g_send, g_recv, v_send, v_recv,
):
    h = lax.axis_index("dp")
    i = lax.axis_index("latent")
    core = lax.rem(i, 2)
    y = lax.rem(i // 2, 4)
    x = lax.rem(i // 8, 4)
    zl = i // 32
    z = 2 * h + zl

    def dev(xx, yy, zz, cc):
        return (zz // 2, ((lax.rem(zz, 2) * 4 + xx) * 4 + yy) * 2 + cc)

    coord = {"x": x, "y": y, "z": z}
    place = {(a, s): mod4(coord[a] + s) for a in coord for s in range(4)}
    near = {}
    for s in range(1, 4):
        near["x", s] = dev(place["x", s], y, z, core)
        near["y", s] = dev(x, place["y", s], z, core)
        near["z", s] = dev(x, y, place["z", s], core)

    def along(axis, step):
        return near[axis, step % 4]

    sibling = dev(x, y, z, 1 - core)
    far_z = 2 * h + 1 - zl
    other_z = dev(x, y, far_z, core)

    def rcopy(src, dst, ssem, rsem, device):
        return pltpu.make_async_remote_copy(
            src_ref=src, dst_ref=dst, send_sem=ssem, recv_sem=rsem,
            device_id=device, device_id_type=MESH,
        )

    def load(j):
        return pltpu.make_async_copy(
            dict_ref.at[:, pl.ds(512 * j, 512)], gacc.at[j], load_sem.at[j]
        )

    first_loads = [
        pltpu.make_async_copy(src, dst, load_sem.at[8 + k])
        for k, (src, dst) in enumerate(
            ((inputs_hbm, inputs_ref), (center_hbm, center_ref), (offset_hbm, offset_ref))
        )
    ]
    for c in first_loads:
        c.start()
    for j in range(8):
        load(j).start()

    column = [
        dev(x, y, place["z", a], c)
        for a in range(4) for b, c in enumerate((core, 1 - core)) if a + b
    ]
    across = {
        axis: [near[axis, a] for a in range(1, 4)]
        + [
            dev(place["x", a], y, far_z, core) if axis == "x" else dev(x, place["y", a], far_z, core)
            for a in range(4)
        ]
        for axis in ("x", "y")
    }
    barrier = pltpu.get_barrier_semaphore()
    partners = column + [d for a in ("x", "y") for d in across[a][:3] + across[a][4:]]
    for partner in partners:
        pl.semaphore_signal(barrier, inc=1, device_id=partner, device_id_type=MESH)

    for c in first_loads:
        c.wait()
    lane = lax.broadcasted_iota(jnp.int32, (1, 128), 1)
    mine = (lane // 64) == core
    both = inputs_ref[...].astype(F32)
    both = jnp.concatenate([both, both], axis=0).T
    raw[...] = jnp.where(mine, both, 0.0).astype(BF16).reshape(2, ROWS, 128)
    cboth = jnp.concatenate([center_ref[...], center_ref[...]], axis=1)
    cen[...] = jnp.broadcast_to(jnp.where(mine, cboth, 0.0), (8, 128))
    pl.semaphore_wait(barrier, len(partners))

    pair = [
        rcopy(raw.at[1 - core], raw_in, pair_send.at[0], pair_recv.at[0], sibling),
        rcopy(cen, cen_in, pair_send.at[1], pair_recv.at[1], sibling),
    ]
    for c in pair:
        c.start()
    for c in pair:
        c.wait_recv()
    center = cen[0:1, :] + cen_in[0:1, :]

    def own_rows(t):
        rows = pl.ds(CHUNK * t, CHUNK)
        return raw[core, rows].astype(F32) + raw_in[rows].astype(F32)

    sent = []

    def flush(log):
        for c in log:
            c.wait_send()
        log.clear()

    orders = (("y", "x", "z"), ("x", "z", "y"), ("z", "y", "x"))
    dirs = ((0, 1), (1, -1))

    def gather(buf, t, block, ssem, rsem, log):
        at = [tuple(coord[a] for a in reversed(o)) for o in orders]
        for p in range(3):
            buf[(t, p) + at[p]] = block[PART * p : PART * (p + 1)]

        def chunk(p, f, step):
            q = place[orders[p][f], step % 4]
            return (t, p) + at[p][: 2 - f] + (q,)

        def send(p, f, e, idx, step):
            ref = buf.at[idx]
            rcopy(
                ref, ref, ssem.at[t, p, f], rsem.at[t, p, e], along(orders[p][f], step)
            ).start()

        def whole(p, f, e, idx):
            ref = buf.at[idx]
            return rcopy(ref, ref, ssem.at[t, p, f], rsem.at[t, p, e], sibling)

        def triple(p, f):
            return (t, p) + at[p][: 2 - f] + (pl.ds(0, 3),)

        def double(p, f):
            return (t, p) + at[p][: 2 - f] + (pl.ds(0, 2),)

        def single(p, f):
            return (t, p) + at[p][: 2 - f] + (0,)

        for p in range(3):
            for step in (1, 3, 2):
                send(p, 0, 0, chunk(p, 0, 0), step)
            log.append(whole(p, 0, 0, triple(p, 0)))
        yield
        for p in range(3):
            whole(p, 0, 0, triple(p, 0)).wait_recv()
            for k, step in dirs:
                send(p, 1, 1, chunk(p, 1, 0), step)
            log.append(whole(p, 1, 1, triple(p, 1)))
        yield
        for p in range(3):
            whole(p, 1, 1, double(p, 1)).wait_recv()
            for k, step in dirs:
                send(p, 1, 2, chunk(p, 1, -step) + (pl.ds(2 * k, 2),), step)
        yield
        for p in range(3):
            whole(p, 1, 2, single(p, 1)).wait_recv()
            for k, step in dirs:
                send(p, 2, 3, chunk(p, 2, 0) + (pl.ds(2 * k, 2),), step)
            log.append(whole(p, 2, 3, triple(p, 2)))
        for p in range(3):
            for k, step in dirs:
                send(p, 2, 4, chunk(p, 2, 0) + (pl.ds(2 - 2 * k, 2),), step)
        yield
        for p in range(3):
            whole(p, 2, 3, single(p, 2)).wait_recv()
            for k, step in dirs:
                send(p, 2, 5, chunk(p, 2, -step) + (pl.ds(2 * k, 2),), step)
        yield
        for e in (4, 5):
            for p in range(3):
                whole(p, 2, e, single(p, 2)).wait_recv()

    def weight_copy(j):
        return rcopy(
            weights.at[0, j], weights.at[1, j], pair_send.at[2], pair_recv.at[2], sibling
        )

    all_weight_copies = rcopy(
        weights.at[0], weights.at[1], pair_send.at[2], pair_recv.at[2], sibling
    )

    small_copy = rcopy(sm, sm_in, pair_send.at[3], pair_recv.at[3], sibling)

    def prepare():
        sq = jnp.zeros((LAT, 1), F32)
        for j in range(8):
            load(j).wait()
            block = gacc[j]
            weights[0, j] = block.astype(BF16)
            weight_copy(j).start()
            sq = sq + jnp.sum(block * block, axis=1, keepdims=True)
        norm = jnp.sqrt(sq + norm_eps)
        sm[...] = jnp.zeros((8, LAT), F32)
        sm[0:1, :] = offset_ref[...]
        sm[1:2, :] = jnp.broadcast_to(norm, (LAT, 128)).T[0:1, :]
        small_copy.start()

    def slab(buf, t, j):
        jz, jx = j // 4, j % 4
        rows = []
        for r in range(2):
            zz = 2 * (h if r == 0 else 1 - h) + jz
            for p in range(3):
                cols = []
                for yy in range(4):
                    idx = ((zz, jx, yy), (yy, zz, jx), (jx, yy, zz))[p]
                    cols.append(buf[(t, p) + idx])
                rows.append(jnp.concatenate(cols, axis=1))
        return jnp.concatenate(rows, axis=0)

    def all_weights(j):
        return jnp.concatenate([weights[0, j], weights[1, j]], axis=0)

    def project(buf, t, half):
        rows = jnp.concatenate([slab(buf, t, 4 * half + jx) for jx in range(4)], axis=1)
        cols = jnp.concatenate([all_weights(4 * half + jx) for jx in range(4)], axis=1)
        return dot_nt(rows, cols)

    def ring_first(src, lead, axis, b_out, b_in, sems, log):
        q = place[axis, 2]
        for k, step in dirs:
            b_out[k][...] = src[lead + (q, pl.ds(2 * k, 2))].astype(BF16)
            c = rcopy(b_out[k], b_in[k], sems[0][k], sems[1][k], along(axis, step))
            c.start()
            log.append(c)

    def ring_second(src, lead, axis, b_out, b_in, a_out, a_in, sems, log):
        for k, step in dirs:
            q = place[axis, step % 4]
            mix, rest = pl.ds(2 * k, 2), pl.ds(2 - 2 * k, 2)
            a_out[k][rest] = src[lead + (q, rest)].astype(BF16)
            rcopy(b_out[k], b_in[k], sems[0][k], sems[1][k], along(axis, step)).wait_recv()
            a_out[k][mix] = (src[lead + (q, mix)] + b_in[k][...].astype(F32)).astype(BF16)
            c = rcopy(a_out[k], a_in[k], sems[0][2 + k], sems[1][2 + k], along(axis, step))
            c.start()
            log.append(c)

    def ring_last(src, lead, axis, a_out, a_in, sems):
        for k, step in dirs:
            rcopy(a_out[k], a_in[k], sems[0][2 + k], sems[1][2 + k], along(axis, step)).wait_recv()
        return src[lead + (coord[axis],)] + a_in[0][...].astype(F32) + a_in[1][...].astype(F32)

    def direct_first(value, axis, out, into, sems, log):
        for k in range(3):
            out[k] = value(place[axis, k + 1]).astype(BF16)
            rcopy(out.at[k], into.at[k], sems[0][0], sems[1][0], along(axis, k + 1)).start()
        log.append(rcopy(out, into, sems[0][0], sems[1][0], sibling))

    def direct_last(value, axis, out, into, sems):
        rcopy(out, into, sems[0][0], sems[1][0], sibling).wait_recv()
        total = value(coord[axis])
        for k in range(3):
            total = total + into[k].astype(F32)
        return total

    def scatter(t, log):
        side_axes = ("x", "y") if t == 0 else ("y", "x")
        axes = (("x", "y"), ("y", "x"), side_axes)

        def some(ref, *lead):
            return [ref.at[lead + (k,)] for k in range(ref.shape[len(lead)])]

        def sems(p, s):
            return (
                [rs_send.at[t, p, 4 * s + e] for e in range(4)],
                [rs_recv.at[t, p, 4 * s + e] for e in range(4)],
            )

        def line_copy(p, e):
            src, dst = (z_out.at[t, p], z_in.at[t, p]) if e is None else (z_out.at[t, p, e], z_in.at[t, p, e])
            device = sibling if e is None else across[axes[p][1]][e]
            return rcopy(src, dst, rs_send.at[t, p, 4], rs_recv.at[t, p, 4], device)

        pair_copy = rcopy(
            y_out.at[t], y_in.at[t], rs_send.at[t, 2, 8], rs_recv.at[t, 2, 8], other_z
        )
        y_out[t] = side[t, 1 - zl].astype(BF16)
        pair_copy.start()
        ring = [
            (part, (t, p), axes[p][0], some(b0_out, t, p), some(b0_in, t, p), some(a0_out, t, p), some(a0_in, t, p), sems(p, 0))
            for p in range(2)
        ]
        for a in ring:
            ring_first(*a[:5], a[7], log)
        yield
        pair_copy.wait_recv()
        side[t, zl] = side[t, zl] + y_in[t].astype(F32)
        wide = (lambda q: side[t, zl, q], axes[2][0], c1_out.at[t], c1_in.at[t], sems(2, 0))
        direct_first(*wide, log)
        for a in ring:
            ring_second(*a, log)
        yield
        here = coord[axes[2][0]]
        side[t, zl, here] = direct_last(*wide)
        thin = (lambda q: side[t, zl, here, q], axes[2][1], c2_out.at[t], c2_in.at[t], sems(2, 1))
        direct_first(*thin, log)
        for p in range(2):
            first = coord[axes[p][0]]
            part[t, p, first] = ring_last(*ring[p][:3], *ring[p][5:])
            for e in range(7):
                a, w = (e + 1, zl) if e < 3 else (e - 3, 1 - zl)
                z_out[t, p, e] = part[t, p, first, place[axes[p][1], a], w].astype(BF16)
                line_copy(p, e).start()
            log.append(line_copy(p, None))
        yield
        out = []
        for p in range(2):
            total = part[t, p, coord[axes[p][0]], coord[axes[p][1]], zl]
            line_copy(p, None).wait_recv()
            for e in range(7):
                total = total + z_in[t, p, e].astype(F32)
            out.append(total)
        out.append(direct_last(*thin))
        log.append(pair_copy)
        result[t] = jnp.concatenate(out, axis=0)

    result, sq, err_sum, act_own, act_all, off_own, off_all = {}, {}, {}, {}, {}, {}, {}
    shared = {}

    def g_copy(j):
        cols = pl.ds(pl.multiple_of(512 * j, 512), 512)
        return rcopy(g_out.at[:, cols], g_in.at[:, cols], g_send.at[0], g_recv.at[0], sibling)

    def gradient(t, first, last):
        @pl.loop(first, last, unroll=2)
        def _(j):
            errs = slab(ge, 0, j)
            if t == 0:
                out = dot(tmat0[...], jnp.concatenate([slab(gx, 0, j), errs[:EARLY]], axis=0))
            else:
                rows = [slab(ge, 1, j), errs[EARLY:], slab(gx, 1, j)]
                out = dot(tmat1[...], jnp.concatenate(rows, axis=0))
            cols = pl.ds(pl.multiple_of(512 * j, 512), 512)
            if t == 0:
                gacc[j] = out[LAT:]
                grad_ref[:, cols] = out[:LAT]
            else:
                g_out[:, cols] = (gacc[j] + out[LAT:]).astype(BF16)
                g_copy(j).start()
                grad_ref[:, cols] = grad_ref[:, cols] + out[:LAT]

    def steps(t):
        centered = (own_rows(t) - center).astype(BF16)
        log_x, log_r, log_e = [], [], []
        yield from gather(gx, t, centered, gx_send, gx_recv, log_x)
        if t == 0:
            all_weight_copies.wait_recv()
            small_copy.wait_recv()
            shared["bias"] = jnp.concatenate([sm[0:1, :], sm_in[0:1, :]], axis=1)
            shared["norms"] = jnp.concatenate([sm[1:2, :], sm_in[1:2, :]], axis=1)
        norms = shared["norms"]
        pre[t] = project(gx, t, 0) + shared["bias"]
        yield
        pre[t] = pre[t] + project(gx, t, 1)
        yield
        acts[t] = jnp.maximum(pre[t], 0.0).astype(BF16)

        @pl.loop(0, 8, unroll=4)
        def _(j):
            jz, jx = j // 4, lax.rem(j, 4)
            out = dot(acts[t, :CHUNK], all_weights(j))
            for yy in range(4):
                cols = slice(128 * yy, 128 * (yy + 1))
                part[t, 0, jx, yy, jz] = out[:MAIN, cols]
                part[t, 1, yy, jx, jz] = out[MAIN : 2 * MAIN, cols]
                if t == 0:
                    side[t, jz, jx, yy] = out[2 * MAIN :, cols]
                else:
                    side[t, jz, yy, jx] = out[2 * MAIN :, cols]

        ready = scatter(t, log_r)
        next(ready)
        flush(log_x)
        act = acts[t]
        act_own[t] = jnp.sum(act[:CHUNK].astype(F32), axis=0, keepdims=True)
        act_all[t] = act_own[t] + jnp.sum(act[CHUNK:].astype(F32), axis=0, keepdims=True)
        if t == 1:
            tmat1[:, :LATE] = jnp.concatenate([act, acts[0, EARLY:]], axis=0).T
        yield
        yield from ready
        err = result[t] + center - own_rows(t)
        sq[t] = jnp.sum(err * err)
        err_sum[t] = jnp.sum(err, axis=0, keepdims=True)
        derr = (2.0 / TOK * err).astype(BF16)
        ready = gather(ge, t, derr, ge_send, ge_recv, log_e)
        next(ready)
        flush(log_r)
        yield
        yield from ready
        sent.extend(log_e)
        dacc[t] = project(ge, t, 0) + sparsity_coeff / TOK * norms
        yield
        dacts = dacc[t] + project(ge, t, 1)
        dpre = jnp.where(pre[t] > 0, dacts, 0.0).astype(BF16)
        if t == 0:
            tmat0[...] = jnp.concatenate([dpre, acts[0, :EARLY]], axis=0).T
        else:
            tmat1[:, LATE:] = dpre.T
        off_own[t] = jnp.sum(dpre[:CHUNK].astype(F32), axis=0, keepdims=True)
        off_all[t] = off_own[t] + jnp.sum(dpre[CHUNK:].astype(F32), axis=0, keepdims=True)
        yield
        if t == 0:
            gradient(0, 0, 4)
            yield
            gradient(0, 4, 8)
            yield

    run = [steps(0), steps(1)]
    plan = "0101010w01001010110101010101010010011"
    for who in plan:
        if who == "w":
            prepare()
        else:
            next(run[int(who)])
    for one in run:
        assert next(one, one) is one
    off = off_own[0] + off_own[1]
    offs = off_all[0] + off_all[1]
    act_tot = act_all[0] + act_all[1]
    spars = jnp.sum((act_own[0] + act_own[1]) * shared["norms"])

    sums[...] = jnp.zeros((2, 8, LAT), F32)
    for k in range(2):
        sums[k, 0:1, :] = offs[:, LAT * k : LAT * (k + 1)]
        sums[k, 1:2, :] = act_tot[:, LAT * k : LAT * (k + 1)]
    sums_copy = rcopy(sums.at[1], sums_in, pair_send.at[4], pair_recv.at[4], sibling)
    sums_copy.start()

    hi = off.astype(BF16)
    rest = off - hi.astype(F32)
    mid = rest.astype(BF16)
    low = (rest - mid.astype(F32)).astype(BF16)
    row = lax.broadcasted_iota(jnp.int32, (16, 512), 0)
    terms = jnp.where(
        row == 0, hi.astype(F32),
        jnp.where(row == 1, mid.astype(F32), jnp.where(row == 2, low.astype(F32), 0.0)),
    ).astype(BF16)
    for j in range(8):
        enc = jnp.sum(dot(terms, all_weights(j)), axis=0, keepdims=True)
        for yy in range(4):
            vx[j % 4, (j // 4) * 4 + yy : (j // 4) * 4 + yy + 1, :] = -enc[:, 128 * yy : 128 * (yy + 1)]
    scalars = jnp.where(lane == 0, sq[0] + sq[1], jnp.where(lane == 1, spars, 0.0))
    for k in range(4):
        vx[k, 8:16, :] = jnp.broadcast_to(scalars, (8, 128))
    sub = lax.broadcasted_iota(jnp.int32, (16, 128), 0)
    vx[x] = vx[x] + jnp.where(sub == zl * 4 + y, 2.0 / TOK * (err_sum[0] + err_sum[1]), 0.0)

    def v_start(k, src, dst, devices):
        for e, device in enumerate(devices):
            rcopy(src(e), dst.at[e], v_send.at[k], v_recv.at[k], device).start()

    def v_done(k, dst):
        return rcopy(dst, dst, v_send.at[k], v_recv.at[k], sibling)

    v_start(0, lambda e: vx.at[place["x", e + 1]], vx_in, across["x"][:3])
    gradient(1, 0, 3)
    v_done(0, vx_in).wait_recv()
    total = vx[x] + vx_in[0] + vx_in[1] + vx_in[2]
    for k in range(4):
        vy[k, 0:1, :] = total[k : k + 1]
        vy[k, 1:2, :] = total[4 + k : 5 + k]
        vy[k, 2:8, :] = total[8:14]
    v_start(1, lambda e: vy.at[place["y", e + 1]], vy_in, across["y"][:3])
    gradient(1, 3, 5)
    v_done(1, vy_in).wait_recv()
    total = vy[y] + vy_in[0] + vy_in[1] + vy_in[2]
    vz[...] = total
    v_start(2, lambda e: vz, vz_in, column)
    gradient(1, 5, 8)
    v_done(2, vz_in).wait_recv()
    for e in range(7):
        total = total + vz_in[e]
    sums_copy.wait_recv()

    small_ref[...] = jnp.zeros((8, LAT), F32)
    small_ref[0:1, :] = sums[0, 0:1, :] + sums_in[0:1, :]
    small_ref[1:2, :] = sparsity_coeff / TOK * (sums[0, 1:2, :] + sums_in[1:2, :]) / sm[1:2, :]
    slot = jnp.where(zl == 0, total[0:1], total[1:2])
    small_ref[2:3, 0:64] = jnp.where(core == 0, slot[:, :64], slot[:, 64:])
    small_ref[3:4, 0:128] = total[2:3]

    flush(sent)
    for c in pair + [all_weight_copies, small_copy, sums_copy]:
        c.wait_send()
    for k, dst in enumerate((vx_in, vy_in, vz_in)):
        v_done(k, dst).wait_send()
    all_g_copies = rcopy(g_out, g_in, g_send.at[0], g_recv.at[0], sibling)
    all_g_copies.wait_recv()
    all_g_copies.wait_send()


def step_kernel(inputs, center, offset, dictionary):
    vm = pltpu.VMEM
    dma = pltpu.SemaphoreType.DMA
    block = (PART, 128)
    main, side = (MAIN, 128), (SIDE, 128)
    return pl.pallas_call(
        kernel,
        out_shape=[
            jax.ShapeDtypeStruct((LAT, WIDTH), F32),
            jax.ShapeDtypeStruct((LAT, WIDTH), BF16),
            jax.ShapeDtypeStruct((8, LAT), F32),
        ],
        in_specs=[pl.BlockSpec(memory_space=pltpu.HBM)] * 4,
        out_specs=[pl.BlockSpec(memory_space=pltpu.VMEM)] * 3,
        scratch_shapes=[
            vm((64, 2 * ROWS), BF16),
            vm((1, 64), F32),
            vm((1, LAT), F32),
            vm((2, 8, LAT, 512), BF16),
            vm((2, 3, 4, 4, 4) + block, BF16),
            vm((2, 3, 4, 4, 4) + block, BF16),
            vm((2, 2 * CHUNK, 512), F32),
            vm((2, 2 * CHUNK, 512), F32),
            vm((2, 2 * CHUNK, 512), BF16),
            vm((512, 480), BF16),
            vm((512, 672), BF16),
            vm((8, LAT, 512), F32),
            vm((2, ROWS, 128), BF16),
            vm((ROWS, 128), BF16),
            vm((8, 128), F32),
            vm((8, 128), F32),
            vm((8, LAT), F32),
            vm((8, LAT), F32),
            vm((2, 8, LAT), F32),
            vm((8, LAT), F32),
            vm((2, 2, 4, 4, 2) + main, F32),
            vm((2, 2, 2, 2, 2) + main, BF16),
            vm((2, 2, 2, 2, 2) + main, BF16),
            vm((2, 2, 2, 4, 2) + main, BF16),
            vm((2, 2, 2, 4, 2) + main, BF16),
            vm((2, 2, 7) + main, BF16),
            vm((2, 2, 7) + main, BF16),
            vm((2, 2, 4, 4) + side, F32),
            vm((2, 4, 4) + side, BF16),
            vm((2, 4, 4) + side, BF16),
            vm((2, 3, 4) + side, BF16),
            vm((2, 3, 4) + side, BF16),
            vm((2, 3) + side, BF16),
            vm((2, 3) + side, BF16),
            vm((LAT, WIDTH), BF16),
            vm((4, 16, 128), F32),
            vm((3, 16, 128), F32),
            vm((4, 8, 128), F32),
            vm((3, 8, 128), F32),
            vm((8, 128), F32),
            vm((7, 8, 128), F32),
            dma((11,)),
            dma((5,)),
            dma((5,)),
            dma((2, 3, 3)),
            dma((2, 3, 6)),
            dma((2, 3, 3)),
            dma((2, 3, 6)),
            dma((2, 3, 9)),
            dma((2, 3, 9)),
            dma((1,)),
            dma((1,)),
            dma((3,)),
            dma((3,)),
        ],
        compiler_params=pltpu.CompilerParams(
            collective_id=0, has_side_effects=True, vmem_limit_bytes=VMEM_LIMIT
        ),
        cost_estimate=pl.CostEstimate(
            flops=12 * 2**30, bytes_accessed=160 * 2**20, transcendentals=0
        ),
        name="step",
    )(*[pltpu.with_memory_space_constraint(v, pltpu.HBM) for v in (inputs, center, offset, dictionary)])


def small_kernel(small, offset, offset_mean, offset_var, center, center_mean, center_var, *outs):
    rows = (
        (offset, small[0:1, :], offset_mean, offset_var),
        (center, small[2:3, 0:64], center_mean, center_var),
    )
    for k, (param, grad, mean, var) in enumerate(rows):
        new = adam_update(param[...], grad, mean[...], var[...])
        for n in range(3):
            outs[3 * k + n][...] = new[n]
    scalars = small[3:4, 0:128]
    lane = lax.broadcasted_iota(jnp.int32, (1, 128), 1)
    weight = jnp.where(lane == 0, 1.0, jnp.where(lane == 1, sparsity_coeff, 0.0))
    outs[6][...] = jnp.sum(scalars * weight, axis=1, keepdims=True) / (TOK * WIDTH)


def small_step(small, *rows):
    shapes = [(1, LAT)] * 3 + [(1, 64)] * 3 + [(1, 1)]
    return pl.pallas_call(
        small_kernel,
        out_shape=[jax.ShapeDtypeStruct(s, F32) for s in shapes],
        in_specs=[pl.BlockSpec(memory_space=pltpu.VMEM)] * 7,
        out_specs=[pl.BlockSpec(memory_space=pltpu.VMEM)] * 7,
        compiler_params=pltpu.CompilerParams(vmem_limit_bytes=2**20),
        name="small",
    )(small, *[r.reshape(1, -1) for r in rows])


def body(
    inputs,
    dictionary,
    offset,
    center,
    dict_mean,
    dict_var,
    offset_mean,
    offset_var,
    center_mean,
    center_var,
):
    grad, shared, small = step_kernel(
        inputs.T, center.reshape(1, -1), offset.reshape(1, -1), dictionary
    )
    g_dict = grad + shared.astype(F32) + small[1][:, None] * dictionary
    fresh_dict, mean_dict, var_dict = adam_update(dictionary, g_dict, dict_mean, dict_var)
    *rows, loss = small_step(
        small, offset, offset_mean, offset_var, center, center_mean, center_var
    )
    fresh_offset, mean_offset, var_offset, fresh_center, mean_center, var_center = [
        r.reshape(-1) for r in rows
    ]
    loss_value = loss.reshape(())
    return (
        fresh_dict,
        fresh_offset,
        fresh_center,
        mean_dict,
        var_dict,
        mean_offset,
        var_offset,
        mean_center,
        var_center,
        loss_value,
    )


def solution(mesh):
    return jax.shard_map(
        body,
        mesh=mesh,
        in_specs=(
            P("dp", "latent"),
            P("latent", None),
            P("latent"),
            P("latent"),
            P("latent", None),
            P("latent", None),
            P("latent"),
            P("latent"),
            P("latent"),
            P("latent"),
        ),
        out_specs=(
            P("latent", None),
            P("latent"),
            P("latent"),
            P("latent", None),
            P("latent", None),
            P("latent"),
            P("latent"),
            P("latent"),
            P("latent"),
            P(),
        ),
        check_vma=False,
    )
```

profile of v0, /device:TPU:1, one launch (start us, length us, event | category | flops | bytes accessed | tf_op | source)
XLA Modules:
  0.0 97.5 jit_solution(7749103308762086675)
XLA Ops:
  0.6 0.0 copy-start
  0.7 0.0 copy-start.1
  0.7 0.0 copy-start.2
  0.7 0.0 copy-start.3
  0.7 0.0 copy-start.4
  0.7 0.0 copy-start.5
  0.7 0.0 copy-start.6
  0.7 0.0 copy-start.7
  0.7 0.0 copy-start.8
  0.7 90.5 %step.1 = (f32[256,4096]{1,0:T(8,128)S(1)}, bf16[256,4096]{1,0:T(8,128)(2,1)S(1)}, f32[8,256]{1,0:T(8,128)S(1)}) custom-call(bf16[64,576]{1,0:T(8,128)(2,1)} %bitcast.24, f32[1,64]{1,0:T(1,128)} %bitcast.19, f32[1,256]{1,0:T(1,128)} %bitcast.15, f32[256,4096]{1,0:T(8,128)} %dict_ref.1), custom_call_target="tpu_custom_call" | custom-call | flops 12884901888 | bytes 167772160 | tf_op jit(solution)/shard_map/step/pallas_call | solution.py:552
  91.2 0.0 copy-done
  91.2 0.0 copy-done.1
  91.2 0.0 copy-done.2
  91.2 0.0 copy-done.3
  91.3 0.0 copy-done.4
  91.3 0.0 copy-done.5
  91.3 0.6 small.1
  91.9 0.0 copy-done.6
  91.9 0.0 copy-done.7
  91.9 0.0 copy-done.8
  91.9 5.6 %fusion.3 = (f32[256,4096]{1,0:T(8,128)}, f32[256,4096]{1,0:T(8,128)}, f32[256,4096]{1,0:T(8,128)}) fusion(f32[256,4096]{1,0:T(8,128)S(1)} %copy-done.6, f32[256]{0:T(256)S(1)} %bitcast.23, f32[256,4096]{1,0:T(8,128)S(1)} %get-tuple-element.20, bf16[256,4096]{1,0:T(8,128)(2,1)S(1)} %get-tuple-element.21, f32[256,4096]{1,0:T(8,128)S(1)} %copy-done.7, ...), kind=kLoop, calls=%fused_computation.5 | loop fusion | flops 17825792 | bytes 31458304 | tf_op jit(solution)/shard_map/sub | solution.py:36
  (1 shorter events, 0.0 us)
Async XLA Ops:
  0.6 90.6 %copy-start = (f32[256]{0:T(256)S(1)}, f32[256]{0:T(256)}, u32[]{:S(2)}) copy-start(f32[256]{0:T(256)} %param.12) | copy-start | bytes 3076
  0.7 90.6 %copy-start.1 = (f32[256]{0:T(256)S(1)}, f32[256]{0:T(256)}, u32[]{:S(2)}) copy-start(f32[256]{0:T(256)} %param.16) | copy-start | bytes 3076
  0.7 90.6 %copy-start.2 = (f32[256]{0:T(256)S(1)}, f32[256]{0:T(256)}, u32[]{:S(2)}) copy-start(f32[256]{0:T(256)} %param.17) | copy-start | bytes 3076
  0.7 90.6 %copy-start.3 = (f32[64]{0:T(128)S(1)}, f32[64]{0:T(128)}, u32[]{:S(2)}) copy-start(f32[64]{0:T(128)} %param.13) | copy-start | bytes 772
  0.7 90.6 %copy-start.4 = (f32[64]{0:T(128)S(1)}, f32[64]{0:T(128)}, u32[]{:S(2)}) copy-start(f32[64]{0:T(128)} %param.18) | copy-start | bytes 772
  0.7 90.6 %copy-start.5 = (f32[64]{0:T(128)S(1)}, f32[64]{0:T(128)}, u32[]{:S(2)}) copy-start(f32[64]{0:T(128)} %param.19) | copy-start | bytes 772
  0.7 91.2 %copy-start.6 = (f32[256,4096]{1,0:T(8,128)S(1)}, f32[256,4096]{1,0:T(8,128)}, u32[]{:S(2)}) copy-start(f32[256,4096]{1,0:T(8,128)} %dict_ref.1) | copy-start | bytes 12582916
  0.7 91.2 %copy-start.7 = (f32[256,4096]{1,0:T(8,128)S(1)}, f32[256,4096]{1,0:T(8,128)}, u32[]{:S(2)}) copy-start(f32[256,4096]{1,0:T(8,128)} %param.14) | copy-start | bytes 12582916
  0.7 91.2 %copy-start.8 = (f32[256,4096]{1,0:T(8,128)S(1)}, f32[256,4096]{1,0:T(8,128)}, u32[]{:S(2)}) copy-start(f32[256,4096]{1,0:T(8,128)} %param.15) | copy-start | bytes 12582916
where the time goes:
time: 97.6 us; the launch traced here: 97.5 us
  Pallas kernels  91.1 us (93%)
  other arithmetic  5.61 us (6%)
    pallas_call x1, Pallas kernels, step_kernel(): pl.pallas_call(kernel, out_shape=[jax.ShapeDtypeStruct((LAT, WIDTH), F32)...  90.5 us
    sub x1, other arithmetic, adam_update(): param - rate * mean_new / (scaled * lax.rsqrt(scaled) + adam_eps)  5.61 us

commit v1 on v0

--- a/solution.py
+++ b/solution.py
@@ -53,12 +53,12 @@
     inputs_hbm, center_hbm, offset_hbm, dict_ref,
     grad_ref, g_in, small_ref,
     inputs_ref, center_ref, offset_ref,
-    weights, gx, ge, pre, dacc, acts, tmat0, tmat1, gacc,
+    weights, gx, ge, pre, dpre_own, acts, tmat0, tmat1, gacc,
     raw, raw_in, cen, cen_in, sm, sm_in, sums, sums_in,
     part, b0_out, b0_in, a0_out, a0_in, z_out, z_in,
     side, y_out, y_in, c1_out, c1_in, c2_out, c2_in,
     g_out,
-    vx, vx_in, vy, vy_in, vz, vz_in,
+    vx, vx_in, vz, vz_in,
     load_sem, pair_send, pair_recv,
     gx_send, gx_recv, ge_send, ge_recv, rs_send, rs_recv,
     g_send, g_recv, v_send, v_recv,
@@ -111,6 +111,9 @@
     for j in range(8):
         load(j).start()
 
+    plane = [
+        dev(place["x", a], place["y", b], z, core) for a in range(4) for b in range(4) if a + b
+    ]
     column = [
         dev(x, y, place["z", a], c)
         for a in range(4) for b, c in enumerate((core, 1 - core)) if a + b
@@ -124,7 +127,7 @@
         for axis in ("x", "y")
     }
     barrier = pltpu.get_barrier_semaphore()
-    partners = column + [d for a in ("x", "y") for d in across[a][:3] + across[a][4:]]
+    partners = plane + column + across["x"][4:] + across["y"][4:]
     for partner in partners:
         pl.semaphore_signal(barrier, inc=1, device_id=partner, device_id_type=MESH)
 
@@ -236,19 +239,26 @@
 
     small_copy = rcopy(sm, sm_in, pair_send.at[3], pair_recv.at[3], sibling)
 
-    def prepare():
-        sq = jnp.zeros((LAT, 1), F32)
-        for j in range(8):
+    def prepare(part):
+        sq = jnp.zeros((LAT, 128), F32)
+        for j in range(4 * part, 4 * part + 4):
             load(j).wait()
             block = gacc[j]
             weights[0, j] = block.astype(BF16)
             weight_copy(j).start()
-            sq = sq + jnp.sum(block * block, axis=1, keepdims=True)
-        norm = jnp.sqrt(sq + norm_eps)
+            for k in range(4):
+                piece = block[:, 128 * k : 128 * (k + 1)]
+                sq = sq + piece * piece
+        squares.append(sq)
+        if part == 0:
+            return
+        norm = jnp.sqrt(jnp.sum(squares[0] + squares[1], axis=1, keepdims=True) + norm_eps)
         sm[...] = jnp.zeros((8, LAT), F32)
         sm[0:1, :] = offset_ref[...]
         sm[1:2, :] = jnp.broadcast_to(norm, (LAT, 128)).T[0:1, :]
         small_copy.start()
+
+    squares = []
 
     def slab(buf, t, j):
         jz, jx = j // 4, j % 4
@@ -266,10 +276,9 @@
     def all_weights(j):
         return jnp.concatenate([weights[0, j], weights[1, j]], axis=0)
 
-    def project(buf, t, half):
-        rows = jnp.concatenate([slab(buf, t, 4 * half + jx) for jx in range(4)], axis=1)
-        cols = jnp.concatenate([all_weights(4 * half + jx) for jx in range(4)], axis=1)
-        return dot_nt(rows, cols)
+    def project(buf, t, which):
+        rows = jnp.concatenate([slab(buf, t, j) for j in range(8)], axis=1)
+        return dot_nt(rows, jnp.concatenate([weights[which, j] for j in range(8)], axis=1))
 
     def ring_first(src, lead, axis, b_out, b_in, sems, log):
         q = place[axis, 2]
@@ -370,7 +379,6 @@
         result[t] = jnp.concatenate(out, axis=0)
 
     result, sq, err_sum, act_own, act_all, off_own, off_all = {}, {}, {}, {}, {}, {}, {}
-    shared = {}
 
     def g_copy(j):
         cols = pl.ds(pl.multiple_of(512 * j, 512), 512)
@@ -398,15 +406,12 @@
         centered = (own_rows(t) - center).astype(BF16)
         log_x, log_r, log_e = [], [], []
         yield from gather(gx, t, centered, gx_send, gx_recv, log_x)
+        pre[t, :, :LAT] = project(gx, t, 0) + sm[0:1, :]
+        yield
         if t == 0:
             all_weight_copies.wait_recv()
             small_copy.wait_recv()
-            shared["bias"] = jnp.concatenate([sm[0:1, :], sm_in[0:1, :]], axis=1)
-            shared["norms"] = jnp.concatenate([sm[1:2, :], sm_in[1:2, :]], axis=1)
-        norms = shared["norms"]
-        pre[t] = project(gx, t, 0) + shared["bias"]
-        yield
-        pre[t] = pre[t] + project(gx, t, 1)
+        pre[t, :, LAT:] = project(gx, t, 1) + sm_in[0:1, :]
         yield
         acts[t] = jnp.maximum(pre[t], 0.0).astype(BF16)
 
@@ -443,10 +448,15 @@
         yield
         yield from ready
         sent.extend(log_e)
-        dacc[t] = project(ge, t, 0) + sparsity_coeff / TOK * norms
-        yield
-        dacts = dacc[t] + project(ge, t, 1)
-        dpre = jnp.where(pre[t] > 0, dacts, 0.0).astype(BF16)
+
+        def backward(which, norm):
+            dacts = project(ge, t, which) + sparsity_coeff / TOK * norm
+            kept = pre[t, :, LAT * which : LAT * (which + 1)] > 0
+            return jnp.where(kept, dacts, 0.0).astype(BF16)
+
+        dpre_own[t] = backward(0, sm[1:2, :])
+        yield
+        dpre = jnp.concatenate([dpre_own[t], backward(1, sm_in[1:2, :])], axis=1)
         if t == 0:
             tmat0[...] = jnp.concatenate([dpre, acts[0, :EARLY]], axis=0).T
         else:
@@ -461,10 +471,10 @@
             yield
 
     run = [steps(0), steps(1)]
-    plan = "0101010w01001010110101010101010010011"
+    plan = "0101u010w01001010110101010101010010011"
     for who in plan:
-        if who == "w":
-            prepare()
+        if who in "uw":
+            prepare("uw".index(who))
         else:
             next(run[int(who)])
     for one in run:
@@ -472,7 +482,8 @@
     off = off_own[0] + off_own[1]
     offs = off_all[0] + off_all[1]
     act_tot = act_all[0] + act_all[1]
-    spars = jnp.sum((act_own[0] + act_own[1]) * shared["norms"])
+    norms = jnp.concatenate([sm[1:2, :], sm_in[1:2, :]], axis=1)
+    spars = jnp.sum((act_own[0] + act_own[1]) * norms)
 
     sums[...] = jnp.zeros((2, 8, LAT), F32)
     for k in range(2):
@@ -493,36 +504,38 @@
     for j in range(8):
         enc = jnp.sum(dot(terms, all_weights(j)), axis=0, keepdims=True)
         for yy in range(4):
-            vx[j % 4, (j // 4) * 4 + yy : (j // 4) * 4 + yy + 1, :] = -enc[:, 128 * yy : 128 * (yy + 1)]
+            vx[(j % 4) * 4 + yy, j // 4 : j // 4 + 1, :] = -enc[:, 128 * yy : 128 * (yy + 1)]
     scalars = jnp.where(lane == 0, sq[0] + sq[1], jnp.where(lane == 1, spars, 0.0))
-    for k in range(4):
-        vx[k, 8:16, :] = jnp.broadcast_to(scalars, (8, 128))
-    sub = lax.broadcasted_iota(jnp.int32, (16, 128), 0)
-    vx[x] = vx[x] + jnp.where(sub == zl * 4 + y, 2.0 / TOK * (err_sum[0] + err_sum[1]), 0.0)
-
-    def v_start(k, src, dst, devices):
-        for e, device in enumerate(devices):
-            rcopy(src(e), dst.at[e], v_send.at[k], v_recv.at[k], device).start()
-
-    def v_done(k, dst):
-        return rcopy(dst, dst, v_send.at[k], v_recv.at[k], sibling)
-
-    v_start(0, lambda e: vx.at[place["x", e + 1]], vx_in, across["x"][:3])
-    gradient(1, 0, 3)
-    v_done(0, vx_in).wait_recv()
-    total = vx[x] + vx_in[0] + vx_in[1] + vx_in[2]
-    for k in range(4):
-        vy[k, 0:1, :] = total[k : k + 1]
-        vy[k, 1:2, :] = total[4 + k : 5 + k]
-        vy[k, 2:8, :] = total[8:14]
-    v_start(1, lambda e: vy.at[place["y", e + 1]], vy_in, across["y"][:3])
-    gradient(1, 3, 5)
-    v_done(1, vy_in).wait_recv()
-    total = vy[y] + vy_in[0] + vy_in[1] + vy_in[2]
+    for k in range(16):
+        vx[k, 2:8, :] = jnp.broadcast_to(scalars, (6, 128))
+    here = x * 4 + y
+    sub = lax.broadcasted_iota(jnp.int32, (8, 128), 0)
+    vx[here] = vx[here] + jnp.where(sub == zl, 2.0 / TOK * (err_sum[0] + err_sum[1]), 0.0)
+
+    def v_plane(e):
+        a, b = (e + 1) // 4, (e + 1) % 4
+        return rcopy(
+            vx.at[place["x", a] * 4 + place["y", b]], vx_in.at[e], v_send.at[0], v_recv.at[0], plane[e]
+        )
+
+    def v_column(e):
+        return rcopy(vz, vz_in.at[e], v_send.at[1], v_recv.at[1], column[e])
+
+    v_planes = rcopy(vx_in, vx_in, v_send.at[0], v_recv.at[0], sibling)
+    v_columns = rcopy(vz_in, vz_in, v_send.at[1], v_recv.at[1], sibling)
+
+    for e in range(15):
+        v_plane(e).start()
+    gradient(1, 0, 4)
+    total = vx[here]
+    v_planes.wait_recv()
+    for e in range(15):
+        total = total + vx_in[e]
     vz[...] = total
-    v_start(2, lambda e: vz, vz_in, column)
-    gradient(1, 5, 8)
-    v_done(2, vz_in).wait_recv()
+    for e in range(7):
+        v_column(e).start()
+    gradient(1, 4, 8)
+    v_columns.wait_recv()
     for e in range(7):
         total = total + vz_in[e]
     sums_copy.wait_recv()
@@ -537,8 +550,8 @@
     flush(sent)
     for c in pair + [all_weight_copies, small_copy, sums_copy]:
         c.wait_send()
-    for k, dst in enumerate((vx_in, vy_in, vz_in)):
-        v_done(k, dst).wait_send()
+    v_planes.wait_send()
+    v_columns.wait_send()
     all_g_copies = rcopy(g_out, g_in, g_send.at[0], g_recv.at[0], sibling)
     all_g_copies.wait_recv()
     all_g_copies.wait_send()
@@ -566,7 +579,7 @@
             vm((2, 3, 4, 4, 4) + block, BF16),
             vm((2, 3, 4, 4, 4) + block, BF16),
             vm((2, 2 * CHUNK, 512), F32),
-            vm((2, 2 * CHUNK, 512), F32),
+            vm((2, 2 * CHUNK, LAT), BF16),
             vm((2, 2 * CHUNK, 512), BF16),
             vm((512, 480), BF16),
             vm((512, 672), BF16),
@@ -594,10 +607,8 @@
             vm((2, 3) + side, BF16),
             vm((2, 3) + side, BF16),
             vm((LAT, WIDTH), BF16),
-            vm((4, 16, 128), F32),
-            vm((3, 16, 128), F32),
-            vm((4, 8, 128), F32),
-            vm((3, 8, 128), F32),
+            vm((16, 8, 128), F32),
+            vm((15, 8, 128), F32),
             vm((8, 128), F32),
             vm((7, 8, 128), F32),
             dma((11,)),
@@ -611,8 +622,8 @@
             dma((2, 3, 9)),
             dma((1,)),
             dma((1,)),
-            dma((3,)),
-            dma((3,)),
+            dma((2,)),
+            dma((2,)),
         ],
         compiler_params=pltpu.CompilerParams(
             collective_id=0, has_side_effects=True, vmem_limit_bytes=VMEM_LIMIT

time: 97.6 us -> 98.6 us (1.010)
  no operation moved by 1% of the time
where the time goes in v1:
time: 98.6 us; the launch traced here: 98.5 us
  Pallas kernels  92 us (93%)
  other arithmetic  5.61 us (6%)
    pallas_call x1, Pallas kernels, step_kernel(): pl.pallas_call(kernel, out_shape=[jax.ShapeDtypeStruct((LAT, WIDTH), F32)...  91.4 us
    sub x1, other arithmetic, adam_update(): param - rate * mean_new / (scaled * lax.rsqrt(scaled) + adam_eps)  5.61 us

profile of v1, /device:TPU:1, one launch (start us, length us, event | category | flops | bytes accessed | tf_op | source)
XLA Modules:
  0.0 98.5 jit_solution(14507240717198455429)
XLA Ops:
  0.6 0.0 copy-start
  0.7 0.0 copy-start.1
  0.7 0.0 copy-start.2
  0.7 0.0 copy-start.3
  0.7 0.0 copy-start.4
  0.7 0.0 copy-start.5
  0.7 0.0 copy-start.6
  0.7 0.0 copy-start.7
  0.7 0.0 copy-start.8
  0.7 91.4 %step.1 = (f32[256,4096]{1,0:T(8,128)S(1)}, bf16[256,4096]{1,0:T(8,128)(2,1)S(1)}, f32[8,256]{1,0:T(8,128)S(1)}) custom-call(bf16[64,576]{1,0:T(8,128)(2,1)} %bitcast.24, f32[1,64]{1,0:T(1,128)} %bitcast.19, f32[1,256]{1,0:T(1,128)} %bitcast.15, f32[256,4096]{1,0:T(8,128)} %dict_ref.1), custom_call_target="tpu_custom_call" | custom-call | flops 12884901888 | bytes 167772160 | tf_op jit(solution)/shard_map/step/pallas_call | solution.py:565
  92.2 0.0 copy-done
  92.2 0.0 copy-done.1
  92.2 0.0 copy-done.2
  92.2 0.0 copy-done.3
  92.2 0.0 copy-done.4
  92.2 0.0 copy-done.5
  92.3 0.6 small.1
  92.9 0.0 copy-done.6
  92.9 0.0 copy-done.7
  92.9 0.0 copy-done.8
  92.9 5.6 %fusion.3 = (f32[256,4096]{1,0:T(8,128)}, f32[256,4096]{1,0:T(8,128)}, f32[256,4096]{1,0:T(8,128)}) fusion(f32[256,4096]{1,0:T(8,128)S(1)} %copy-done.6, f32[256]{0:T(256)S(1)} %bitcast.23, f32[256,4096]{1,0:T(8,128)S(1)} %get-tuple-element.20, bf16[256,4096]{1,0:T(8,128)(2,1)S(1)} %get-tuple-element.21, f32[256,4096]{1,0:T(8,128)S(1)} %copy-done.7, ...), kind=kLoop, calls=%fused_computation.5 | loop fusion | flops 17825792 | bytes 31458304 | tf_op jit(solution)/shard_map/sub | solution.py:36
  (1 shorter events, 0.0 us)
Async XLA Ops:
  0.6 91.6 %copy-start = (f32[256]{0:T(256)S(1)}, f32[256]{0:T(256)}, u32[]{:S(2)}) copy-start(f32[256]{0:T(256)} %param.12) | copy-start | bytes 3076
  0.7 91.6 %copy-start.1 = (f32[256]{0:T(256)S(1)}, f32[256]{0:T(256)}, u32[]{:S(2)}) copy-start(f32[256]{0:T(256)} %param.16) | copy-start | bytes 3076
  0.7 91.6 %copy-start.2 = (f32[256]{0:T(256)S(1)}, f32[256]{0:T(256)}, u32[]{:S(2)}) copy-start(f32[256]{0:T(256)} %param.17) | copy-start | bytes 3076
  0.7 91.6 %copy-start.3 = (f32[64]{0:T(128)S(1)}, f32[64]{0:T(128)}, u32[]{:S(2)}) copy-start(f32[64]{0:T(128)} %param.13) | copy-start | bytes 772
  0.7 91.6 %copy-start.4 = (f32[64]{0:T(128)S(1)}, f32[64]{0:T(128)}, u32[]{:S(2)}) copy-start(f32[64]{0:T(128)} %param.18) | copy-start | bytes 772
  0.7 91.6 %copy-start.5 = (f32[64]{0:T(128)S(1)}, f32[64]{0:T(128)}, u32[]{:S(2)}) copy-start(f32[64]{0:T(128)} %param.19) | copy-start | bytes 772
  0.7 92.1 %copy-start.6 = (f32[256,4096]{1,0:T(8,128)S(1)}, f32[256,4096]{1,0:T(8,128)}, u32[]{:S(2)}) copy-start(f32[256,4096]{1,0:T(8,128)} %dict_ref.1) | copy-start | bytes 12582916
  0.7 92.1 %copy-start.7 = (f32[256,4096]{1,0:T(8,128)S(1)}, f32[256,4096]{1,0:T(8,128)}, u32[]{:S(2)}) copy-start(f32[256,4096]{1,0:T(8,128)} %param.14) | copy-start | bytes 12582916
  0.7 92.1 %copy-start.8 = (f32[256,4096]{1,0:T(8,128)S(1)}, f32[256,4096]{1,0:T(8,128)}, u32[]{:S(2)}) copy-start(f32[256,4096]{1,0:T(8,128)} %param.15) | copy-start | bytes 12582916

commit v2 on v1

--- a/solution.py
+++ b/solution.py
@@ -20,8 +20,6 @@
 PART = 48
 MAIN, SIDE = 64, 16
 LAT = 256
-EARLY = 192
-LATE = 384
 VMEM_LIMIT = 40 * 1024 * 1024
 F32 = jnp.float32
 BF16 = jnp.bfloat16
@@ -53,7 +51,7 @@
     inputs_hbm, center_hbm, offset_hbm, dict_ref,
     grad_ref, g_in, small_ref,
     inputs_ref, center_ref, offset_ref,
-    weights, gx, ge, pre, dpre_own, acts, tmat0, tmat1, gacc,
+    weights, gx, ge, pre, dacc, acts, tmat, gacc,
     raw, raw_in, cen, cen_in, sm, sm_in, sums, sums_in,
     part, b0_out, b0_in, a0_out, a0_in, z_out, z_in,
     side, y_out, y_in, c1_out, c1_in, c2_out, c2_in,
@@ -239,26 +237,19 @@
 
     small_copy = rcopy(sm, sm_in, pair_send.at[3], pair_recv.at[3], sibling)
 
-    def prepare(part):
-        sq = jnp.zeros((LAT, 128), F32)
-        for j in range(4 * part, 4 * part + 4):
+    def prepare():
+        sq = jnp.zeros((LAT, 1), F32)
+        for j in range(8):
             load(j).wait()
             block = gacc[j]
             weights[0, j] = block.astype(BF16)
             weight_copy(j).start()
-            for k in range(4):
-                piece = block[:, 128 * k : 128 * (k + 1)]
-                sq = sq + piece * piece
-        squares.append(sq)
-        if part == 0:
-            return
-        norm = jnp.sqrt(jnp.sum(squares[0] + squares[1], axis=1, keepdims=True) + norm_eps)
+            sq = sq + jnp.sum(block * block, axis=1, keepdims=True)
+        norm = jnp.sqrt(sq + norm_eps)
         sm[...] = jnp.zeros((8, LAT), F32)
         sm[0:1, :] = offset_ref[...]
         sm[1:2, :] = jnp.broadcast_to(norm, (LAT, 128)).T[0:1, :]
         small_copy.start()
-
-    squares = []
 
     def slab(buf, t, j):
         jz, jx = j // 4, j % 4
@@ -276,9 +267,10 @@
     def all_weights(j):
         return jnp.concatenate([weights[0, j], weights[1, j]], axis=0)
 
-    def project(buf, t, which):
-        rows = jnp.concatenate([slab(buf, t, j) for j in range(8)], axis=1)
-        return dot_nt(rows, jnp.concatenate([weights[which, j] for j in range(8)], axis=1))
+    def project(buf, t, half):
+        rows = jnp.concatenate([slab(buf, t, 4 * half + jx) for jx in range(4)], axis=1)
+        cols = jnp.concatenate([all_weights(4 * half + jx) for jx in range(4)], axis=1)
+        return dot_nt(rows, cols)
 
     def ring_first(src, lead, axis, b_out, b_in, sems, log):
         q = place[axis, 2]
@@ -379,6 +371,7 @@
         result[t] = jnp.concatenate(out, axis=0)
 
     result, sq, err_sum, act_own, act_all, off_own, off_all = {}, {}, {}, {}, {}, {}, {}
+    shared = {}
 
     def g_copy(j):
         cols = pl.ds(pl.multiple_of(512 * j, 512), 512)
@@ -387,12 +380,7 @@
     def gradient(t, first, last):
         @pl.loop(first, last, unroll=2)
         def _(j):
-            errs = slab(ge, 0, j)
-            if t == 0:
-                out = dot(tmat0[...], jnp.concatenate([slab(gx, 0, j), errs[:EARLY]], axis=0))
-            else:
-                rows = [slab(ge, 1, j), errs[EARLY:], slab(gx, 1, j)]
-                out = dot(tmat1[...], jnp.concatenate(rows, axis=0))
+            out = dot(tmat[t], jnp.concatenate([slab(gx, t, j), slab(ge, t, j)], axis=0))
             cols = pl.ds(pl.multiple_of(512 * j, 512), 512)
             if t == 0:
                 gacc[j] = out[LAT:]
@@ -406,12 +394,15 @@
         centered = (own_rows(t) - center).astype(BF16)
         log_x, log_r, log_e = [], [], []
         yield from gather(gx, t, centered, gx_send, gx_recv, log_x)
-        pre[t, :, :LAT] = project(gx, t, 0) + sm[0:1, :]
-        yield
         if t == 0:
             all_weight_copies.wait_recv()
             small_copy.wait_recv()
-        pre[t, :, LAT:] = project(gx, t, 1) + sm_in[0:1, :]
+            shared["bias"] = jnp.concatenate([sm[0:1, :], sm_in[0:1, :]], axis=1)
+            shared["norms"] = jnp.concatenate([sm[1:2, :], sm_in[1:2, :]], axis=1)
+        norms = shared["norms"]
+        pre[t] = project(gx, t, 0) + shared["bias"]
+        yield
+        pre[t] = pre[t] + project(gx, t, 1)
         yield
         acts[t] = jnp.maximum(pre[t], 0.0).astype(BF16)
 
@@ -434,8 +425,6 @@
         act = acts[t]
         act_own[t] = jnp.sum(act[:CHUNK].astype(F32), axis=0, keepdims=True)
         act_all[t] = act_own[t] + jnp.sum(act[CHUNK:].astype(F32), axis=0, keepdims=True)
-        if t == 1:
-            tmat1[:, :LATE] = jnp.concatenate([act, acts[0, EARLY:]], axis=0).T
         yield
         yield from ready
         err = result[t] + center - own_rows(t)
@@ -448,19 +437,11 @@
         yield
         yield from ready
         sent.extend(log_e)
-
-        def backward(which, norm):
-            dacts = project(ge, t, which) + sparsity_coeff / TOK * norm
-            kept = pre[t, :, LAT * which : LAT * (which + 1)] > 0
-            return jnp.where(kept, dacts, 0.0).astype(BF16)
-
-        dpre_own[t] = backward(0, sm[1:2, :])
-        yield
-        dpre = jnp.concatenate([dpre_own[t], backward(1, sm_in[1:2, :])], axis=1)
-        if t == 0:
-            tmat0[...] = jnp.concatenate([dpre, acts[0, :EARLY]], axis=0).T
-        else:
-            tmat1[:, LATE:] = dpre.T
+        dacc[t] = project(ge, t, 0) + sparsity_coeff / TOK * norms
+        yield
+        dacts = dacc[t] + project(ge, t, 1)
+        dpre = jnp.where(pre[t] > 0, dacts, 0.0).astype(BF16)
+        tmat[t] = jnp.concatenate([dpre, acts[t]], axis=0).T
         off_own[t] = jnp.sum(dpre[:CHUNK].astype(F32), axis=0, keepdims=True)
         off_all[t] = off_own[t] + jnp.sum(dpre[CHUNK:].astype(F32), axis=0, keepdims=True)
         yield
@@ -471,10 +452,10 @@
             yield
 
     run = [steps(0), steps(1)]
-    plan = "0101u010w01001010110101010101010010011"
+    plan = "0101010w01001010110101010101010010011"
     for who in plan:
-        if who in "uw":
-            prepare("uw".index(who))
+        if who == "w":
+            prepare()
         else:
             next(run[int(who)])
     for one in run:
@@ -482,8 +463,7 @@
     off = off_own[0] + off_own[1]
     offs = off_all[0] + off_all[1]
     act_tot = act_all[0] + act_all[1]
-    norms = jnp.concatenate([sm[1:2, :], sm_in[1:2, :]], axis=1)
-    spars = jnp.sum((act_own[0] + act_own[1]) * norms)
+    spars = jnp.sum((act_own[0] + act_own[1]) * shared["norms"])
 
     sums[...] = jnp.zeros((2, 8, LAT), F32)
     for k in range(2):
@@ -579,10 +559,9 @@
             vm((2, 3, 4, 4, 4) + block, BF16),
             vm((2, 3, 4, 4, 4) + block, BF16),
             vm((2, 2 * CHUNK, 512), F32),
-            vm((2, 2 * CHUNK, LAT), BF16),
+            vm((2, 2 * CHUNK, 512), F32),
             vm((2, 2 * CHUNK, 512), BF16),
-            vm((512, 480), BF16),
-            vm((512, 672), BF16),
+            vm((2, 512, 4 * CHUNK), BF16),
             vm((8, LAT, 512), F32),
             vm((2, ROWS, 128), BF16),
             vm((ROWS, 128), BF16),

time: 98.6 us -> 96.9 us (0.983)
  Pallas kernels: 92 us -> 90.4 us
    pallas_call x1, Pallas kernels: 91.4 us -> 89.8 us  [step_kernel(): pl.pallas_call(kernel, out_shape=[jax.ShapeDtypeStruct((LAT, WIDTH), F32)...]
where the time goes in v2:
time: 96.9 us; the launch traced here: 96.8 us
  Pallas kernels  90.4 us (93%)
  other arithmetic  5.61 us (6%)
    pallas_call x1, Pallas kernels, step_kernel(): pl.pallas_call(kernel, out_shape=[jax.ShapeDtypeStruct((LAT, WIDTH), F32)...  89.8 us
    sub x1, other arithmetic, adam_update(): param - rate * mean_new / (scaled * lax.rsqrt(scaled) + adam_eps)  5.61 us

profile of v2, /device:TPU:1, one launch (start us, length us, event | category | flops | bytes accessed | tf_op | source)
XLA Modules:
  0.0 96.8 jit_solution(10934572354870042565)
XLA Ops:
  0.6 0.0 copy-start
  0.7 0.0 copy-start.1
  0.7 0.0 copy-start.2
  0.7 0.0 copy-start.3
  0.7 0.0 copy-start.4
  0.7 0.0 copy-start.5
  0.7 0.0 copy-start.6
  0.7 0.0 copy-start.7
  0.7 0.0 copy-start.8
  0.7 89.8 %step.1 = (f32[256,4096]{1,0:T(8,128)S(1)}, bf16[256,4096]{1,0:T(8,128)(2,1)S(1)}, f32[8,256]{1,0:T(8,128)S(1)}) custom-call(bf16[64,576]{1,0:T(8,128)(2,1)} %bitcast.24, f32[1,64]{1,0:T(1,128)} %bitcast.19, f32[1,256]{1,0:T(1,128)} %bitcast.15, f32[256,4096]{1,0:T(8,128)} %dict_ref.1), custom_call_target="tpu_custom_call" | custom-call | flops 12884901888 | bytes 167772160 | tf_op jit(solution)/shard_map/step/pallas_call | solution.py:545
  90.5 0.0 copy-done
  90.5 0.0 copy-done.1
  90.6 0.0 copy-done.2
  90.6 0.0 copy-done.3
  90.6 0.0 copy-done.4
  90.6 0.0 copy-done.5
  90.6 0.6 small.1
  91.2 0.0 copy-done.6
  91.2 0.0 copy-done.7
  91.2 0.0 copy-done.8
  91.2 5.6 %fusion.3 = (f32[256,4096]{1,0:T(8,128)}, f32[256,4096]{1,0:T(8,128)}, f32[256,4096]{1,0:T(8,128)}) fusion(f32[256,4096]{1,0:T(8,128)S(1)} %copy-done.6, f32[256]{0:T(256)S(1)} %bitcast.23, f32[256,4096]{1,0:T(8,128)S(1)} %get-tuple-element.20, bf16[256,4096]{1,0:T(8,128)(2,1)S(1)} %get-tuple-element.21, f32[256,4096]{1,0:T(8,128)S(1)} %copy-done.7, ...), kind=kLoop, calls=%fused_computation.5 | loop fusion | flops 17825792 | bytes 31458304 | tf_op jit(solution)/shard_map/sub | solution.py:34
  (1 shorter events, 0.0 us)
Async XLA Ops:
  0.6 89.9 %copy-start = (f32[256]{0:T(256)S(1)}, f32[256]{0:T(256)}, u32[]{:S(2)}) copy-start(f32[256]{0:T(256)} %param.12) | copy-start | bytes 3076
  0.7 89.9 %copy-start.1 = (f32[256]{0:T(256)S(1)}, f32[256]{0:T(256)}, u32[]{:S(2)}) copy-start(f32[256]{0:T(256)} %param.16) | copy-start | bytes 3076
  0.7 89.9 %copy-start.2 = (f32[256]{0:T(256)S(1)}, f32[256]{0:T(256)}, u32[]{:S(2)}) copy-start(f32[256]{0:T(256)} %param.17) | copy-start | bytes 3076
  0.7 89.9 %copy-start.3 = (f32[64]{0:T(128)S(1)}, f32[64]{0:T(128)}, u32[]{:S(2)}) copy-start(f32[64]{0:T(128)} %param.13) | copy-start | bytes 772
  0.7 89.9 %copy-start.4 = (f32[64]{0:T(128)S(1)}, f32[64]{0:T(128)}, u32[]{:S(2)}) copy-start(f32[64]{0:T(128)} %param.18) | copy-start | bytes 772
  0.7 89.9 %copy-start.5 = (f32[64]{0:T(128)S(1)}, f32[64]{0:T(128)}, u32[]{:S(2)}) copy-start(f32[64]{0:T(128)} %param.19) | copy-start | bytes 772
  0.7 90.5 %copy-start.6 = (f32[256,4096]{1,0:T(8,128)S(1)}, f32[256,4096]{1,0:T(8,128)}, u32[]{:S(2)}) copy-start(f32[256,4096]{1,0:T(8,128)} %dict_ref.1) | copy-start | bytes 12582916
  0.7 90.5 %copy-start.7 = (f32[256,4096]{1,0:T(8,128)S(1)}, f32[256,4096]{1,0:T(8,128)}, u32[]{:S(2)}) copy-start(f32[256,4096]{1,0:T(8,128)} %param.14) | copy-start | bytes 12582916
  0.7 90.5 %copy-start.8 = (f32[256,4096]{1,0:T(8,128)S(1)}, f32[256,4096]{1,0:T(8,128)}, u32[]{:S(2)}) copy-start(f32[256,4096]{1,0:T(8,128)} %param.15) | copy-start | bytes 12582916

commit v3 on v2

--- a/solution.py
+++ b/solution.py
@@ -251,14 +251,14 @@
         sm[1:2, :] = jnp.broadcast_to(norm, (LAT, 128)).T[0:1, :]
         small_copy.start()
 
-    def slab(buf, t, j):
+    def slab(buf, t, j, blocks=(0, 1, 2, 3)):
         jz, jx = j // 4, j % 4
         rows = []
         for r in range(2):
             zz = 2 * (h if r == 0 else 1 - h) + jz
             for p in range(3):
                 cols = []
-                for yy in range(4):
+                for yy in blocks:
                     idx = ((zz, jx, yy), (yy, zz, jx), (jx, yy, zz))[p]
                     cols.append(buf[(t, p) + idx])
                 rows.append(jnp.concatenate(cols, axis=1))
@@ -378,17 +378,22 @@
         return rcopy(g_out.at[:, cols], g_in.at[:, cols], g_send.at[0], g_recv.at[0], sibling)
 
     def gradient(t, first, last):
-        @pl.loop(first, last, unroll=2)
+        @pl.loop(first, last)
         def _(j):
-            out = dot(tmat[t], jnp.concatenate([slab(gx, t, j), slab(ge, t, j)], axis=0))
-            cols = pl.ds(pl.multiple_of(512 * j, 512), 512)
-            if t == 0:
-                gacc[j] = out[LAT:]
-                grad_ref[:, cols] = out[:LAT]
-            else:
-                g_out[:, cols] = (gacc[j] + out[LAT:]).astype(BF16)
+            for k in range(2):
+                blocks = (2 * k, 2 * k + 1)
+                both = jnp.concatenate([slab(gx, t, j, blocks), slab(ge, t, j, blocks)], axis=0)
+                out = dot(tmat[t], both)
+                half = slice(256 * k, 256 * (k + 1))
+                cols = pl.ds(pl.multiple_of(512 * j + 256 * k, 256), 256)
+                if t == 0:
+                    gacc[j, :, half] = out[LAT:]
+                    grad_ref[:, cols] = out[:LAT]
+                else:
+                    g_out[:, cols] = (gacc[j, :, half] + out[LAT:]).astype(BF16)
+                    grad_ref[:, cols] = grad_ref[:, cols] + out[:LAT]
+            if t == 1:
                 g_copy(j).start()
-                grad_ref[:, cols] = grad_ref[:, cols] + out[:LAT]
 
     def steps(t):
         centered = (own_rows(t) - center).astype(BF16)

time: 96.9 us -> 97.3 us (level)
  no operation moved by 1% of the time
where the time goes in v3:
time: 97.3 us; the launch traced here: 97.2 us
  Pallas kernels  90.8 us (93%)
  other arithmetic  5.61 us (6%)
    pallas_call x1, Pallas kernels, step_kernel(): pl.pallas_call(kernel, out_shape=[jax.ShapeDtypeStruct((LAT, WIDTH), F32)...  90.2 us
    sub x1, other arithmetic, adam_update(): param - rate * mean_new / (scaled * lax.rsqrt(scaled) + adam_eps)  5.61 us

profile of v3, /device:TPU:1, one launch (start us, length us, event | category | flops | bytes accessed | tf_op | source)
XLA Modules:
  0.0 97.2 jit_solution(1627904111919089246)
XLA Ops:
  0.6 0.0 copy-start
  0.7 0.0 copy-start.1
  0.7 0.0 copy-start.2
  0.7 0.0 copy-start.3
  0.7 0.0 copy-start.4
  0.7 0.0 copy-start.5
  0.7 0.0 copy-start.6
  0.7 0.0 copy-start.7
  0.7 0.0 copy-start.8
  0.7 90.2 %step.1 = (f32[256,4096]{1,0:T(8,128)S(1)}, bf16[256,4096]{1,0:T(8,128)(2,1)S(1)}, f32[8,256]{1,0:T(8,128)S(1)}) custom-call(bf16[64,576]{1,0:T(8,128)(2,1)} %bitcast.24, f32[1,64]{1,0:T(1,128)} %bitcast.19, f32[1,256]{1,0:T(1,128)} %bitcast.15, f32[256,4096]{1,0:T(8,128)} %dict_ref.1), custom_call_target="tpu_custom_call" | custom-call | flops 12884901888 | bytes 167772160 | tf_op jit(solution)/shard_map/step/pallas_call | solution.py:550
  91.0 0.0 copy-done
  91.0 0.0 copy-done.1
  91.0 0.0 copy-done.2
  91.0 0.0 copy-done.3
  91.0 0.0 copy-done.4
  91.0 0.0 copy-done.5
  91.0 0.6 small.1
  91.6 0.0 copy-done.6
  91.6 0.0 copy-done.7
  91.6 0.0 copy-done.8
  91.6 5.6 %fusion.3 = (f32[256,4096]{1,0:T(8,128)}, f32[256,4096]{1,0:T(8,128)}, f32[256,4096]{1,0:T(8,128)}) fusion(f32[256,4096]{1,0:T(8,128)S(1)} %copy-done.6, f32[256]{0:T(256)S(1)} %bitcast.23, f32[256,4096]{1,0:T(8,128)S(1)} %get-tuple-element.20, bf16[256,4096]{1,0:T(8,128)(2,1)S(1)} %get-tuple-element.21, f32[256,4096]{1,0:T(8,128)S(1)} %copy-done.7, ...), kind=kLoop, calls=%fused_computation.5 | loop fusion | flops 17825792 | bytes 31458304 | tf_op jit(solution)/shard_map/sub | solution.py:34
  (1 shorter events, 0.0 us)
Async XLA Ops:
  0.6 90.3 %copy-start = (f32[256]{0:T(256)S(1)}, f32[256]{0:T(256)}, u32[]{:S(2)}) copy-start(f32[256]{0:T(256)} %param.12) | copy-start | bytes 3076
  0.7 90.3 %copy-start.1 = (f32[256]{0:T(256)S(1)}, f32[256]{0:T(256)}, u32[]{:S(2)}) copy-start(f32[256]{0:T(256)} %param.16) | copy-start | bytes 3076
  0.7 90.3 %copy-start.2 = (f32[256]{0:T(256)S(1)}, f32[256]{0:T(256)}, u32[]{:S(2)}) copy-start(f32[256]{0:T(256)} %param.17) | copy-start | bytes 3076
  0.7 90.3 %copy-start.3 = (f32[64]{0:T(128)S(1)}, f32[64]{0:T(128)}, u32[]{:S(2)}) copy-start(f32[64]{0:T(128)} %param.13) | copy-start | bytes 772
  0.7 90.3 %copy-start.4 = (f32[64]{0:T(128)S(1)}, f32[64]{0:T(128)}, u32[]{:S(2)}) copy-start(f32[64]{0:T(128)} %param.18) | copy-start | bytes 772
  0.7 90.3 %copy-start.5 = (f32[64]{0:T(128)S(1)}, f32[64]{0:T(128)}, u32[]{:S(2)}) copy-start(f32[64]{0:T(128)} %param.19) | copy-start | bytes 772
  0.7 90.9 %copy-start.6 = (f32[256,4096]{1,0:T(8,128)S(1)}, f32[256,4096]{1,0:T(8,128)}, u32[]{:S(2)}) copy-start(f32[256,4096]{1,0:T(8,128)} %dict_ref.1) | copy-start | bytes 12582916
  0.7 90.9 %copy-start.7 = (f32[256,4096]{1,0:T(8,128)S(1)}, f32[256,4096]{1,0:T(8,128)}, u32[]{:S(2)}) copy-start(f32[256,4096]{1,0:T(8,128)} %param.14) | copy-start | bytes 12582916
  0.7 90.9 %copy-start.8 = (f32[256,4096]{1,0:T(8,128)S(1)}, f32[256,4096]{1,0:T(8,128)}, u32[]{:S(2)}) copy-start(f32[256,4096]{1,0:T(8,128)} %param.15) | copy-start | bytes 12582916

commit v4 on v3

--- a/solution.py
+++ b/solution.py
@@ -51,8 +51,8 @@
     inputs_hbm, center_hbm, offset_hbm, dict_ref,
     grad_ref, g_in, small_ref,
     inputs_ref, center_ref, offset_ref,
-    weights, gx, ge, pre, dacc, acts, tmat, gacc,
-    raw, raw_in, cen, cen_in, sm, sm_in, sums, sums_in,
+    weights, gx, ge, pre, dacc, acts, act_t, dpre_t, gacc,
+    raw, raw_in, cen, cen_in, sm, sm_in, stat, sums, sums_in,
     part, b0_out, b0_in, a0_out, a0_in, z_out, z_in,
     side, y_out, y_in, c1_out, c1_in, c2_out, c2_in,
     g_out,
@@ -246,9 +246,8 @@
             weight_copy(j).start()
             sq = sq + jnp.sum(block * block, axis=1, keepdims=True)
         norm = jnp.sqrt(sq + norm_eps)
-        sm[...] = jnp.zeros((8, LAT), F32)
-        sm[0:1, :] = offset_ref[...]
-        sm[1:2, :] = jnp.broadcast_to(norm, (LAT, 128)).T[0:1, :]
+        offset = jnp.broadcast_to(offset_ref[...], (128, LAT)).T
+        sm[...] = jnp.where(lane == 0, offset, jnp.where(lane == 1, norm, 0.0))
         small_copy.start()
 
     def slab(buf, t, j, blocks=(0, 1, 2, 3)):
@@ -270,7 +269,7 @@
     def project(buf, t, half):
         rows = jnp.concatenate([slab(buf, t, 4 * half + jx) for jx in range(4)], axis=1)
         cols = jnp.concatenate([all_weights(4 * half + jx) for jx in range(4)], axis=1)
-        return dot_nt(rows, cols)
+        return dot_nt(cols, rows)
 
     def ring_first(src, lead, axis, b_out, b_in, sems, log):
         q = place[axis, 2]
@@ -370,8 +369,11 @@
         log.append(pair_copy)
         result[t] = jnp.concatenate(out, axis=0)
 
-    result, sq, err_sum, act_own, act_all, off_own, off_all = {}, {}, {}, {}, {}, {}, {}
-    shared = {}
+    result, sq, err_sum = {}, {}, {}
+    own_lane = lax.broadcasted_iota(jnp.int32, (1, 2 * CHUNK), 1) < CHUNK
+    def column_of(k):
+        return jnp.concatenate([sm[:, k : k + 1], sm_in[:, k : k + 1]], axis=0)
+
 
     def g_copy(j):
         cols = pl.ds(pl.multiple_of(512 * j, 512), 512)
@@ -382,8 +384,7 @@
         def _(j):
             for k in range(2):
                 blocks = (2 * k, 2 * k + 1)
-                both = jnp.concatenate([slab(gx, t, j, blocks), slab(ge, t, j, blocks)], axis=0)
-                out = dot(tmat[t], both)
+                out = dot(dpre_t[t], slab(gx, t, j, blocks)) + dot(act_t[t], slab(ge, t, j, blocks))
                 half = slice(256 * k, 256 * (k + 1))
                 cols = pl.ds(pl.multiple_of(512 * j + 256 * k, 256), 256)
                 if t == 0:
@@ -402,19 +403,18 @@
         if t == 0:
             all_weight_copies.wait_recv()
             small_copy.wait_recv()
-            shared["bias"] = jnp.concatenate([sm[0:1, :], sm_in[0:1, :]], axis=1)
-            shared["norms"] = jnp.concatenate([sm[1:2, :], sm_in[1:2, :]], axis=1)
-        norms = shared["norms"]
-        pre[t] = project(gx, t, 0) + shared["bias"]
+        pre[t] = project(gx, t, 0) + column_of(0)
         yield
         pre[t] = pre[t] + project(gx, t, 1)
         yield
-        acts[t] = jnp.maximum(pre[t], 0.0).astype(BF16)
+        act = jnp.maximum(pre[t], 0.0).astype(BF16)
+        act_t[t] = act
+        acts[t] = act.T[:CHUNK]
 
         @pl.loop(0, 8, unroll=4)
         def _(j):
             jz, jx = j // 4, lax.rem(j, 4)
-            out = dot(acts[t, :CHUNK], all_weights(j))
+            out = dot(acts[t], all_weights(j))
             for yy in range(4):
                 cols = slice(128 * yy, 128 * (yy + 1))
                 part[t, 0, jx, yy, jz] = out[:MAIN, cols]
@@ -427,9 +427,10 @@
         ready = scatter(t, log_r)
         next(ready)
         flush(log_x)
-        act = acts[t]
-        act_own[t] = jnp.sum(act[:CHUNK].astype(F32), axis=0, keepdims=True)
-        act_all[t] = act_own[t] + jnp.sum(act[CHUNK:].astype(F32), axis=0, keepdims=True)
+        wide = act_t[t].astype(F32)
+        act_own = jnp.sum(jnp.where(own_lane, wide, 0.0), axis=1, keepdims=True)
+        act_all = jnp.sum(wide, axis=1, keepdims=True)
+        stat[t] = jnp.where(lane == 0, act_own, jnp.where(lane == 1, act_all, 0.0))
         yield
         yield from ready
         err = result[t] + center - own_rows(t)
@@ -442,13 +443,15 @@
         yield
         yield from ready
         sent.extend(log_e)
-        dacc[t] = project(ge, t, 0) + sparsity_coeff / TOK * norms
+        dacc[t] = project(ge, t, 0) + sparsity_coeff / TOK * column_of(1)
         yield
         dacts = dacc[t] + project(ge, t, 1)
         dpre = jnp.where(pre[t] > 0, dacts, 0.0).astype(BF16)
-        tmat[t] = jnp.concatenate([dpre, acts[t]], axis=0).T
-        off_own[t] = jnp.sum(dpre[:CHUNK].astype(F32), axis=0, keepdims=True)
-        off_all[t] = off_own[t] + jnp.sum(dpre[CHUNK:].astype(F32), axis=0, keepdims=True)
+        dpre_t[t] = dpre
+        wide = dpre.astype(F32)
+        off_own = jnp.sum(jnp.where(own_lane, wide, 0.0), axis=1, keepdims=True)
+        off_all = jnp.sum(wide, axis=1, keepdims=True)
+        stat[t] = stat[t] + jnp.where(lane == 2, off_own, jnp.where(lane == 3, off_all, 0.0))
         yield
         if t == 0:
             gradient(0, 0, 4)
@@ -465,10 +468,10 @@
             next(run[int(who)])
     for one in run:
         assert next(one, one) is one
-    off = off_own[0] + off_own[1]
-    offs = off_all[0] + off_all[1]
-    act_tot = act_all[0] + act_all[1]
-    spars = jnp.sum((act_own[0] + act_own[1]) * shared["norms"])
+    rows = (stat[0] + stat[1]).T
+    act_row, act_tot, off, offs = [rows[k : k + 1] for k in range(4)]
+    norms = jnp.concatenate([sm[...].T[1:2], sm_in[...].T[1:2]], axis=1)
+    spars = jnp.sum(act_row * norms)
 
     sums[...] = jnp.zeros((2, 8, LAT), F32)
     for k in range(2):
@@ -527,7 +530,7 @@
 
     small_ref[...] = jnp.zeros((8, LAT), F32)
     small_ref[0:1, :] = sums[0, 0:1, :] + sums_in[0:1, :]
-    small_ref[1:2, :] = sparsity_coeff / TOK * (sums[0, 1:2, :] + sums_in[1:2, :]) / sm[1:2, :]
+    small_ref[1:2, :] = sparsity_coeff / TOK * (sums[0, 1:2, :] + sums_in[1:2, :]) / norms[:, :LAT]
     slot = jnp.where(zl == 0, total[0:1], total[1:2])
     small_ref[2:3, 0:64] = jnp.where(core == 0, slot[:, :64], slot[:, 64:])
     small_ref[3:4, 0:128] = total[2:3]
@@ -563,17 +566,19 @@
             vm((2, 8, LAT, 512), BF16),
             vm((2, 3, 4, 4, 4) + block, BF16),
             vm((2, 3, 4, 4, 4) + block, BF16),
-            vm((2, 2 * CHUNK, 512), F32),
-            vm((2, 2 * CHUNK, 512), F32),
-            vm((2, 2 * CHUNK, 512), BF16),
-            vm((2, 512, 4 * CHUNK), BF16),
+            vm((2, 512, 2 * CHUNK), F32),
+            vm((2, 512, 2 * CHUNK), F32),
+            vm((2, CHUNK, 512), BF16),
+            vm((2, 512, 2 * CHUNK), BF16),
+            vm((2, 512, 2 * CHUNK), BF16),
             vm((8, LAT, 512), F32),
             vm((2, ROWS, 128), BF16),
             vm((ROWS, 128), BF16),
             vm((8, 128), F32),
             vm((8, 128), F32),
-            vm((8, LAT), F32),
-            vm((8, LAT), F32),
+            vm((LAT, 128), F32),
+            vm((LAT, 128), F32),
+            vm((2, 2 * LAT, 128), F32),
             vm((2, 8, LAT), F32),
             vm((8, LAT), F32),
             vm((2, 2, 4, 4, 2) + main, F32),

time: 97.3 us -> 101 us (1.038)
  Pallas kernels: 90.8 us -> 94.2 us
    pallas_call x1, Pallas kernels: 90.2 us -> 93.6 us  [step_kernel(): pl.pallas_call(kernel, out_shape=[jax.ShapeDtypeStruct((LAT, WIDTH), F32)...]
where the time goes in v4:
time: 101 us
  Pallas kernels  94.2 us (93%)
  other arithmetic  5.61 us (6%)
    pallas_call x1, Pallas kernels, step_kernel(): pl.pallas_call(kernel, out_shape=[jax.ShapeDtypeStruct((LAT, WIDTH), F32)...  93.6 us
    sub x1, other arithmetic, adam_update(): param - rate * mean_new / (scaled * lax.rsqrt(scaled) + adam_eps)  5.61 us

profile of v4, /device:TPU:1, one launch (start us, length us, event | category | flops | bytes accessed | tf_op | source)
XLA Modules:
  0.0 100.6 jit_solution(677047528759829714)
XLA Ops:
  0.6 0.0 copy-start
  0.7 0.0 copy-start.1
  0.7 0.0 copy-start.2
  0.7 0.0 copy-start.3
  0.7 0.0 copy-start.4
  0.7 0.0 copy-start.5
  0.7 0.0 copy-start.6
  0.7 0.0 copy-start.7
  0.7 0.0 copy-start.8
  0.7 93.6 %step.1 = (f32[256,4096]{1,0:T(8,128)S(1)}, bf16[256,4096]{1,0:T(8,128)(2,1)S(1)}, f32[8,256]{1,0:T(8,128)S(1)}) custom-call(bf16[64,576]{1,0:T(8,128)(2,1)} %bitcast.24, f32[1,64]{1,0:T(1,128)} %bitcast.19, f32[1,256]{1,0:T(1,128)} %bitcast.15, f32[256,4096]{1,0:T(8,128)} %dict_ref.1), custom_call_target="tpu_custom_call" | custom-call | flops 12884901888 | bytes 167772160 | tf_op jit(solution)/shard_map/step/pallas_call | solution.py:553
  94.4 0.0 copy-done
  94.4 0.0 copy-done.1
  94.4 0.0 copy-done.2
  94.4 0.0 copy-done.3
  94.4 0.0 copy-done.4
  94.4 0.0 copy-done.5
  94.4 0.6 small.1
  95.0 0.0 copy-done.6
  95.0 0.0 copy-done.7
  95.0 0.0 copy-done.8
  95.0 5.6 %fusion.3 = (f32[256,4096]{1,0:T(8,128)}, f32[256,4096]{1,0:T(8,128)}, f32[256,4096]{1,0:T(8,128)}) fusion(f32[256,4096]{1,0:T(8,128)S(1)} %copy-done.6, f32[256]{0:T(256)S(1)} %bitcast.23, f32[256,4096]{1,0:T(8,128)S(1)} %get-tuple-element.20, bf16[256,4096]{1,0:T(8,128)(2,1)S(1)} %get-tuple-element.21, f32[256,4096]{1,0:T(8,128)S(1)} %copy-done.7, ...), kind=kLoop, calls=%fused_computation.5 | loop fusion | flops 17825792 | bytes 31458304 | tf_op jit(solution)/shard_map/sub | solution.py:34
  (1 shorter events, 0.0 us)
Async XLA Ops:
  0.6 93.7 %copy-start = (f32[256]{0:T(256)S(1)}, f32[256]{0:T(256)}, u32[]{:S(2)}) copy-start(f32[256]{0:T(256)} %param.12) | copy-start | bytes 3076
  0.7 93.7 %copy-start.1 = (f32[256]{0:T(256)S(1)}, f32[256]{0:T(256)}, u32[]{:S(2)}) copy-start(f32[256]{0:T(256)} %param.16) | copy-start | bytes 3076
  0.7 93.7 %copy-start.2 = (f32[256]{0:T(256)S(1)}, f32[256]{0:T(256)}, u32[]{:S(2)}) copy-start(f32[256]{0:T(256)} %param.17) | copy-start | bytes 3076
  0.7 93.7 %copy-start.3 = (f32[64]{0:T(128)S(1)}, f32[64]{0:T(128)}, u32[]{:S(2)}) copy-start(f32[64]{0:T(128)} %param.13) | copy-start | bytes 772
  0.7 93.7 %copy-start.4 = (f32[64]{0:T(128)S(1)}, f32[64]{0:T(128)}, u32[]{:S(2)}) copy-start(f32[64]{0:T(128)} %param.18) | copy-start | bytes 772
  0.7 93.7 %copy-start.5 = (f32[64]{0:T(128)S(1)}, f32[64]{0:T(128)}, u32[]{:S(2)}) copy-start(f32[64]{0:T(128)} %param.19) | copy-start | bytes 772
  0.7 94.3 %copy-start.6 = (f32[256,4096]{1,0:T(8,128)S(1)}, f32[256,4096]{1,0:T(8,128)}, u32[]{:S(2)}) copy-start(f32[256,4096]{1,0:T(8,128)} %dict_ref.1) | copy-start | bytes 12582916
  0.7 94.3 %copy-start.7 = (f32[256,4096]{1,0:T(8,128)S(1)}, f32[256,4096]{1,0:T(8,128)}, u32[]{:S(2)}) copy-start(f32[256,4096]{1,0:T(8,128)} %param.14) | copy-start | bytes 12582916
  0.7 94.3 %copy-start.8 = (f32[256,4096]{1,0:T(8,128)S(1)}, f32[256,4096]{1,0:T(8,128)}, u32[]{:S(2)}) copy-start(f32[256,4096]{1,0:T(8,128)} %param.15) | copy-start | bytes 12582916

commit v5 on v3

--- a/solution.py
+++ b/solution.py
@@ -457,7 +457,7 @@
             yield
 
     run = [steps(0), steps(1)]
-    plan = "0101010w01001010110101010101010010011"
+    plan = "0101010w01001010110101010101010100011"
     for who in plan:
         if who == "w":
             prepare()

time: 97.3 us -> 98.3 us (1.010)
  no operation moved by 1% of the time
where the time goes in v5:
time: 98.3 us; the launch traced here: 98.2 us
  Pallas kernels  91.7 us (93%)
  other arithmetic  5.61 us (6%)
    pallas_call x1, Pallas kernels, step_kernel(): pl.pallas_call(kernel, out_shape=[jax.ShapeDtypeStruct((LAT, WIDTH), F32)...  91.1 us
    sub x1, other arithmetic, adam_update(): param - rate * mean_new / (scaled * lax.rsqrt(scaled) + adam_eps)  5.61 us

profile of v5, /device:TPU:1, one launch (start us, length us, event | category | flops | bytes accessed | tf_op | source)
XLA Modules:
  0.0 98.2 jit_solution(12085710110819767796)
XLA Ops:
  0.6 0.0 copy-start
  0.7 0.0 copy-start.1
  0.7 0.0 copy-start.2
  0.7 0.0 copy-start.3
  0.7 0.0 copy-start.4
  0.7 0.0 copy-start.5
  0.7 0.0 copy-start.6
  0.7 0.0 copy-start.7
  0.7 0.0 copy-start.8
  0.7 91.1 %step.1 = (f32[256,4096]{1,0:T(8,128)S(1)}, bf16[256,4096]{1,0:T(8,128)(2,1)S(1)}, f32[8,256]{1,0:T(8,128)S(1)}) custom-call(bf16[64,576]{1,0:T(8,128)(2,1)} %bitcast.24, f32[1,64]{1,0:T(1,128)} %bitcast.19, f32[1,256]{1,0:T(1,128)} %bitcast.15, f32[256,4096]{1,0:T(8,128)} %dict_ref.1), custom_call_target="tpu_custom_call" | custom-call | flops 12884901888 | bytes 167772160 | tf_op jit(solution)/shard_map/step/pallas_call | solution.py:550
  91.9 0.0 copy-done
  91.9 0.0 copy-done.1
  91.9 0.0 copy-done.2
  91.9 0.0 copy-done.3
  91.9 0.0 copy-done.4
  91.9 0.0 copy-done.5
  92.0 0.6 small.1
  92.5 0.0 copy-done.6
  92.6 0.0 copy-done.7
  92.6 0.0 copy-done.8
  92.6 5.6 %fusion.3 = (f32[256,4096]{1,0:T(8,128)}, f32[256,4096]{1,0:T(8,128)}, f32[256,4096]{1,0:T(8,128)}) fusion(f32[256,4096]{1,0:T(8,128)S(1)} %copy-done.6, f32[256]{0:T(256)S(1)} %bitcast.23, f32[256,4096]{1,0:T(8,128)S(1)} %get-tuple-element.20, bf16[256,4096]{1,0:T(8,128)(2,1)S(1)} %get-tuple-element.21, f32[256,4096]{1,0:T(8,128)S(1)} %copy-done.7, ...), kind=kLoop, calls=%fused_computation.5 | loop fusion | flops 17825792 | bytes 31458304 | tf_op jit(solution)/shard_map/sub | solution.py:34
  (1 shorter events, 0.0 us)
Async XLA Ops:
  0.6 91.2 %copy-start = (f32[256]{0:T(256)S(1)}, f32[256]{0:T(256)}, u32[]{:S(2)}) copy-start(f32[256]{0:T(256)} %param.12) | copy-start | bytes 3076
  0.7 91.2 %copy-start.1 = (f32[256]{0:T(256)S(1)}, f32[256]{0:T(256)}, u32[]{:S(2)}) copy-start(f32[256]{0:T(256)} %param.16) | copy-start | bytes 3076
  0.7 91.2 %copy-start.2 = (f32[256]{0:T(256)S(1)}, f32[256]{0:T(256)}, u32[]{:S(2)}) copy-start(f32[256]{0:T(256)} %param.17) | copy-start | bytes 3076
  0.7 91.2 %copy-start.3 = (f32[64]{0:T(128)S(1)}, f32[64]{0:T(128)}, u32[]{:S(2)}) copy-start(f32[64]{0:T(128)} %param.13) | copy-start | bytes 772
  0.7 91.2 %copy-start.4 = (f32[64]{0:T(128)S(1)}, f32[64]{0:T(128)}, u32[]{:S(2)}) copy-start(f32[64]{0:T(128)} %param.18) | copy-start | bytes 772
  0.7 91.2 %copy-start.5 = (f32[64]{0:T(128)S(1)}, f32[64]{0:T(128)}, u32[]{:S(2)}) copy-start(f32[64]{0:T(128)} %param.19) | copy-start | bytes 772
  0.7 91.8 %copy-start.6 = (f32[256,4096]{1,0:T(8,128)S(1)}, f32[256,4096]{1,0:T(8,128)}, u32[]{:S(2)}) copy-start(f32[256,4096]{1,0:T(8,128)} %dict_ref.1) | copy-start | bytes 12582916
  0.7 91.8 %copy-start.7 = (f32[256,4096]{1,0:T(8,128)S(1)}, f32[256,4096]{1,0:T(8,128)}, u32[]{:S(2)}) copy-start(f32[256,4096]{1,0:T(8,128)} %param.14) | copy-start | bytes 12582916
  0.7 91.8 %copy-start.8 = (f32[256,4096]{1,0:T(8,128)S(1)}, f32[256,4096]{1,0:T(8,128)}, u32[]{:S(2)}) copy-start(f32[256,4096]{1,0:T(8,128)} %param.15) | copy-start | bytes 12582916

commit v6 on v5

--- a/solution.py
+++ b/solution.py
@@ -457,7 +457,7 @@
             yield
 
     run = [steps(0), steps(1)]
-    plan = "0101010w01001010110101010101010100011"
+    plan = "0101010w01001010110101010101010001011"
     for who in plan:
         if who == "w":
             prepare()

time: 98.3 us -> 99.1 us (level)
  no operation moved by 1% of the time
where the time goes in v6:
time: 99.1 us; the launch traced here: 99 us
  Pallas kernels  92.5 us (93%)
  other arithmetic  5.61 us (6%)
    pallas_call x1, Pallas kernels, step_kernel(): pl.pallas_call(kernel, out_shape=[jax.ShapeDtypeStruct((LAT, WIDTH), F32)...  91.9 us
    sub x1, other arithmetic, adam_update(): param - rate * mean_new / (scaled * lax.rsqrt(scaled) + adam_eps)  5.61 us

profile of v6, /device:TPU:1, one launch (start us, length us, event | category | flops | bytes accessed | tf_op | source)
XLA Modules:
  0.0 99.0 jit_solution(10246789960721545843)
XLA Ops:
  0.6 0.0 copy-start
  0.7 0.0 copy-start.1
  0.7 0.0 copy-start.2
  0.7 0.0 copy-start.3
  0.7 0.0 copy-start.4
  0.7 0.0 copy-start.5
  0.7 0.0 copy-start.6
  0.7 0.0 copy-start.7
  0.7 0.0 copy-start.8
  0.7 91.9 %step.1 = (f32[256,4096]{1,0:T(8,128)S(1)}, bf16[256,4096]{1,0:T(8,128)(2,1)S(1)}, f32[8,256]{1,0:T(8,128)S(1)}) custom-call(bf16[64,576]{1,0:T(8,128)(2,1)} %bitcast.24, f32[1,64]{1,0:T(1,128)} %bitcast.19, f32[1,256]{1,0:T(1,128)} %bitcast.15, f32[256,4096]{1,0:T(8,128)} %dict_ref.1), custom_call_target="tpu_custom_call" | custom-call | flops 12884901888 | bytes 167772160 | tf_op jit(solution)/shard_map/step/pallas_call | solution.py:550
  92.7 0.0 copy-done
  92.7 0.0 copy-done.1
  92.7 0.0 copy-done.2
  92.7 0.0 copy-done.3
  92.7 0.0 copy-done.4
  92.7 0.0 copy-done.5
  92.7 0.6 small.1
  93.3 0.0 copy-done.6
  93.3 0.0 copy-done.7
  93.3 0.0 copy-done.8
  93.4 5.6 %fusion.3 = (f32[256,4096]{1,0:T(8,128)}, f32[256,4096]{1,0:T(8,128)}, f32[256,4096]{1,0:T(8,128)}) fusion(f32[256,4096]{1,0:T(8,128)S(1)} %copy-done.6, f32[256]{0:T(256)S(1)} %bitcast.23, f32[256,4096]{1,0:T(8,128)S(1)} %get-tuple-element.20, bf16[256,4096]{1,0:T(8,128)(2,1)S(1)} %get-tuple-element.21, f32[256,4096]{1,0:T(8,128)S(1)} %copy-done.7, ...), kind=kLoop, calls=%fused_computation.5 | loop fusion | flops 17825792 | bytes 31458304 | tf_op jit(solution)/shard_map/sub | solution.py:34
  (1 shorter events, 0.0 us)
Async XLA Ops:
  0.6 92.0 %copy-start = (f32[256]{0:T(256)S(1)}, f32[256]{0:T(256)}, u32[]{:S(2)}) copy-start(f32[256]{0:T(256)} %param.12) | copy-start | bytes 3076
  0.7 92.0 %copy-start.1 = (f32[256]{0:T(256)S(1)}, f32[256]{0:T(256)}, u32[]{:S(2)}) copy-start(f32[256]{0:T(256)} %param.16) | copy-start | bytes 3076
  0.7 92.0 %copy-start.2 = (f32[256]{0:T(256)S(1)}, f32[256]{0:T(256)}, u32[]{:S(2)}) copy-start(f32[256]{0:T(256)} %param.17) | copy-start | bytes 3076
  0.7 92.0 %copy-start.3 = (f32[64]{0:T(128)S(1)}, f32[64]{0:T(128)}, u32[]{:S(2)}) copy-start(f32[64]{0:T(128)} %param.13) | copy-start | bytes 772
  0.7 92.0 %copy-start.4 = (f32[64]{0:T(128)S(1)}, f32[64]{0:T(128)}, u32[]{:S(2)}) copy-start(f32[64]{0:T(128)} %param.18) | copy-start | bytes 772
  0.7 92.0 %copy-start.5 = (f32[64]{0:T(128)S(1)}, f32[64]{0:T(128)}, u32[]{:S(2)}) copy-start(f32[64]{0:T(128)} %param.19) | copy-start | bytes 772
  0.7 92.6 %copy-start.6 = (f32[256,4096]{1,0:T(8,128)S(1)}, f32[256,4096]{1,0:T(8,128)}, u32[]{:S(2)}) copy-start(f32[256,4096]{1,0:T(8,128)} %dict_ref.1) | copy-start | bytes 12582916
  0.7 92.6 %copy-start.7 = (f32[256,4096]{1,0:T(8,128)S(1)}, f32[256,4096]{1,0:T(8,128)}, u32[]{:S(2)}) copy-start(f32[256,4096]{1,0:T(8,128)} %param.14) | copy-start | bytes 12582916
  0.7 92.6 %copy-start.8 = (f32[256,4096]{1,0:T(8,128)S(1)}, f32[256,4096]{1,0:T(8,128)}, u32[]{:S(2)}) copy-start(f32[256,4096]{1,0:T(8,128)} %param.15) | copy-start | bytes 12582916
